TPU v7x, 32 devices: a whole 2x2x4 slice. The times are simulated.
32 devices in a mesh: dp: 2 (over x), ctx: 8 (over z, core), tensor: 2 (over y).
Axes of the slice: x: 2, y: 2, z: 4, core: 2. Of those that a mesh axis runs over, the one named last changes fastest.
Arguments:
- inputs: bfloat16 [16, 2, 8, 64, 512], P('dp', None, 'ctx'), may hold values from -6 to 6
- cotangent: bfloat16 [16, 2, 8, 64, 512], P('dp', None, 'ctx'), may hold values from -6 to 6
- live_frames: int32 [16], P('dp'), may hold values from 1 to 16, as said below
- gain_attn: float32 [512], replicated, may hold values from 0.5 to 1.5
- shift_attn: float32 [512], replicated, may hold values from -3 to 3
- w_qkv: bfloat16 [512, 8, 192], P(None, 'tensor'), may hold values from -0.25 to 0.25
- w_out: bfloat16 [512, 512], P('tensor'), may hold values from -4 to 4
- gain_mlp: float32 [512], replicated, may hold values from 0.5 to 1.5
- shift_mlp: float32 [512], replicated, may hold values from -3 to 3
- w_up: bfloat16 [512, 2048], P(None, 'tensor'), may hold values from -0.25 to 0.25
- up_bias: float32 [2048], P('tensor'), may hold values from -3 to 3
- w_down: bfloat16 [2048, 512], P('tensor'), may hold values from -0.125 to 0.125
Outputs:
- output: bfloat16 [16, 2, 8, 64, 512], P('dp', None, 'ctx')
- input_grad: bfloat16 [16, 2, 8, 64, 512], P('dp', None, 'ctx')
- grad_gain_attn: float32 [512], P('tensor')
- grad_shift_attn: float32 [512], P('tensor')
- grad_qkv: float32 [512, 8, 192], P(None, 'tensor')
- grad_out: float32 [512, 512], P('tensor')
- grad_gain_mlp: float32 [512], P('tensor')
- grad_shift_mlp: float32 [512], P('tensor')
- grad_up: float32 [512, 2048], P(None, 'tensor')
- grad_up_bias: float32 [2048], P('tensor')
- grad_down: float32 [2048, 512], P('tensor')
Inputs may be any that keep to these rules, and one draw needn't show every extreme that they name: `live_frames`: in the 8 clips of one index of dp, one clip, drawn from the seed, has all 16 frames live.
All inputs are finite; a program needn't handle non-finite values.
Results may differ from a plain program's by a relative error of at most 0.022.
Values may be sent and summed in bfloat16 or wider, within the bound.
A program may use at most 128 MiB of HBM per device.

v0:
```python
from functools import partial

import jax
import jax.numpy as jnp
from jax import lax
from jax.sharding import PartitionSpec as P

PATCH = 64


EPSILON = 1e-05


def layer_norm(values, norm_gain, norm_shift):
    row_mean = jnp.mean(values, axis=-1, keepdims=True)
    centered = values - row_mean
    variance = jnp.mean(centered * centered, axis=-1, keepdims=True)
    return centered * lax.rsqrt(variance + EPSILON) * norm_gain + norm_shift


def attention_scores(queries, key_part, allowed, score_scale):
    scores = (
        jnp.einsum("cqhd,ckhd->chqk", queries, key_part, preferred_element_type=jnp.float32)
        * score_scale
    )
    return jnp.where(allowed[:, None], scores, -1e30)


def body(
    inputs,
    cotangent,
    live_frames,
    gain_attn,
    shift_attn,
    w_qkv,
    w_out,
    gain_mlp,
    shift_mlp,
    w_up,
    up_bias,
    w_down,
):
    clip_count = inputs.shape[0]
    block_len = inputs.shape[3]
    model_width = inputs.shape[4]
    heads_here = w_qkv.shape[1]
    head_dim = w_qkv.shape[2] // 3
    pair_width = heads_here * 2 * head_dim
    score_scale = head_dim ** (-0.5)
    ctx_count = lax.axis_size("ctx")
    ctx_index = lax.axis_index("ctx")
    frame_blocks = block_len // PATCH
    flat_rows = inputs.reshape(-1, model_width).astype(jnp.float32)
    normed, norm_pull = jax.vjp(layer_norm, flat_rows, gain_attn, shift_attn)
    normed_low = normed.astype(jnp.bfloat16)
    packed = jnp.dot(
        normed_low, w_qkv.reshape(model_width, -1), preferred_element_type=jnp.float32
    ).astype(jnp.bfloat16)
    packed = packed.reshape(clip_count, 2, block_len, heads_here, 3 * head_dim)
    queries = packed[..., :head_dim].reshape(clip_count, 2 * block_len, heads_here, head_dim)
    pairs = packed[..., head_dim:].reshape(clip_count, 2, 1, block_len, pair_width)
    token_frame = jnp.arange(block_len) // PATCH
    slot_index = jnp.arange(ctx_count)
    gathered = lax.all_gather(pairs, "ctx", axis=2, tiled=True)
    block_ids = jnp.stack([slot_index, 2 * ctx_count - 1 - slot_index])
    key_frame = (block_ids[:, :, None] * frame_blocks + token_frame[None, None, :]).reshape(-1)
    keyset = gathered.reshape(clip_count, -1, heads_here, 2 * head_dim)
    key_part = keyset[..., :head_dim]
    value_part = keyset[..., head_dim:]
    query_frame = jnp.concatenate(
        [
            ctx_index * frame_blocks + token_frame,
            (2 * ctx_count - 1 - ctx_index) * frame_blocks + token_frame,
        ]
    )
    allowed = (key_frame[None, None, :] <= query_frame[None, :, None]) & (
        key_frame[None, None, :] < live_frames[:, None, None]
    )
    scores = attention_scores(queries, key_part, allowed, score_scale)
    row_top = jnp.max(scores, axis=-1, keepdims=True)
    weights = jnp.exp(scores - row_top)
    row_total = jnp.sum(weights, axis=-1, keepdims=True)
    log_total = row_top + jnp.log(row_total)
    attn_probs = weights / row_total
    mixed = jnp.einsum(
        "chqk,ckhd->cqhd",
        attn_probs.astype(jnp.bfloat16),
        value_part,
        preferred_element_type=jnp.float32,
    ).astype(jnp.bfloat16)
    mixed_flat = mixed.reshape(-1, heads_here * head_dim)
    attn_out = lax.psum(jnp.dot(mixed_flat, w_out, preferred_element_type=jnp.float32), "tensor")
    middle = flat_rows + attn_out
    second, second_pull = jax.vjp(layer_norm, middle, gain_mlp, shift_mlp)
    second_low = second.astype(jnp.bfloat16)
    pre_act = jnp.dot(second_low, w_up, preferred_element_type=jnp.float32) + up_bias
    activated, gelu_pull = jax.vjp(partial(jax.nn.gelu, approximate=True), pre_act)
    activated_low = activated.astype(jnp.bfloat16)
    mlp_out = lax.psum(
        jnp.dot(activated_low, w_down, preferred_element_type=jnp.float32).astype(jnp.bfloat16),
        "tensor",
    ).astype(jnp.float32)
    output = (middle + mlp_out).astype(jnp.bfloat16).reshape(inputs.shape)
    share = model_width // lax.axis_size("tensor")
    begin = lax.axis_index("tensor") * share

    def own_slice(vector):
        return lax.dynamic_slice_in_dim(vector, begin, share)

    upstream = cotangent.reshape(-1, model_width)
    grad_act = jnp.einsum("rd,fd->rf", upstream, w_down, preferred_element_type=jnp.float32)
    grad_pre = gelu_pull(grad_act)[0].astype(jnp.bfloat16)
    grad_down = jnp.einsum("rf,rd->fd", activated_low, upstream, preferred_element_type=jnp.float32)
    grad_up = jnp.einsum("rd,rf->df", second_low, grad_pre, preferred_element_type=jnp.float32)
    grad_up_bias = jnp.sum(grad_pre.astype(jnp.float32), axis=0)
    grad_second = lax.psum(
        jnp.einsum("rf,df->rd", grad_pre, w_up, preferred_element_type=jnp.float32).astype(
            jnp.bfloat16
        ),
        "tensor",
    ).astype(jnp.float32)
    grad_middle_ln, grad_gain_mlp, grad_shift_mlp = second_pull(grad_second)
    grad_middle = upstream.astype(jnp.float32) + grad_middle_ln
    middle_low = grad_middle.astype(jnp.bfloat16)
    grad_out = jnp.einsum("rk,rd->kd", mixed_flat, middle_low, preferred_element_type=jnp.float32)
    grad_mixed = jnp.einsum(
        "rd,kd->rk", middle_low, w_out, preferred_element_type=jnp.float32
    ).astype(jnp.bfloat16)
    grad_mixed = grad_mixed.reshape(clip_count, 2 * block_len, heads_here, head_dim)
    scores = attention_scores(queries, key_part, allowed, score_scale)
    attn_probs = jnp.exp(scores - log_total)
    grad_probs = jnp.einsum(
        "cqhd,ckhd->chqk", grad_mixed, value_part, preferred_element_type=jnp.float32
    )
    row_delta = jnp.sum(grad_probs * attn_probs, axis=-1, keepdims=True)
    grad_scores = (attn_probs * (grad_probs - row_delta)).astype(jnp.bfloat16)
    grad_query = (
        jnp.einsum("chqk,ckhd->cqhd", grad_scores, key_part, preferred_element_type=jnp.float32)
        * score_scale
    ).astype(jnp.bfloat16)
    grad_keys = (
        jnp.einsum("chqk,cqhd->ckhd", grad_scores, queries, preferred_element_type=jnp.float32)
        * score_scale
    )
    grad_values = jnp.einsum(
        "chqk,cqhd->ckhd",
        attn_probs.astype(jnp.bfloat16),
        grad_mixed,
        preferred_element_type=jnp.float32,
    )
    grad_pairs = jnp.concatenate([grad_keys, grad_values], axis=-1)
    grad_shaped = grad_pairs.reshape(clip_count, 2, ctx_count, block_len, pair_width)
    owned = (
        lax.psum_scatter(grad_shaped.astype(jnp.bfloat16), "ctx", scatter_dimension=2, tiled=True)
        .astype(jnp.float32)
        .reshape(clip_count, 2, block_len, pair_width)
    )
    owned_low = owned.astype(jnp.bfloat16).reshape(
        clip_count, 2, block_len, heads_here, 2 * head_dim
    )
    grad_packed = jnp.concatenate(
        [grad_query.reshape(clip_count, 2, block_len, heads_here, head_dim), owned_low], axis=-1
    )
    grad_packed = grad_packed.reshape(-1, heads_here * 3 * head_dim)
    grad_qkv = jnp.einsum(
        "rd,rk->dk", normed_low, grad_packed, preferred_element_type=jnp.float32
    ).reshape(w_qkv.shape)
    grad_normed = lax.psum(
        jnp.einsum(
            "rk,dk->rd",
            grad_packed,
            w_qkv.reshape(model_width, -1),
            preferred_element_type=jnp.float32,
        ).astype(jnp.bfloat16),
        "tensor",
    ).astype(jnp.float32)
    grad_flat_ln, grad_gain_attn, grad_shift_attn = norm_pull(grad_normed)
    input_grad = (grad_middle + grad_flat_ln).astype(jnp.bfloat16).reshape(inputs.shape)
    summed = (
        lax.psum(grad_qkv.astype(jnp.bfloat16), ("dp", "ctx")).astype(jnp.float32),
        lax.psum(grad_out.astype(jnp.bfloat16), ("dp", "ctx")).astype(jnp.float32),
        lax.psum(own_slice(grad_gain_attn).astype(jnp.bfloat16), ("dp", "ctx")).astype(jnp.float32),
        lax.psum(own_slice(grad_shift_attn).astype(jnp.bfloat16), ("dp", "ctx")).astype(
            jnp.float32
        ),
        lax.psum(grad_up.astype(jnp.bfloat16), ("dp", "ctx")).astype(jnp.float32),
        lax.psum(grad_up_bias.astype(jnp.bfloat16), ("dp", "ctx")).astype(jnp.float32),
        lax.psum(grad_down.astype(jnp.bfloat16), ("dp", "ctx")).astype(jnp.float32),
        lax.psum(own_slice(grad_gain_mlp).astype(jnp.bfloat16), ("dp", "ctx")).astype(jnp.float32),
        lax.psum(own_slice(grad_shift_mlp).astype(jnp.bfloat16), ("dp", "ctx")).astype(jnp.float32),
    )
    return (
        output,
        input_grad,
        summed[2],
        summed[3],
        summed[0],
        summed[1],
        summed[7],
        summed[8],
        summed[4],
        summed[5],
        summed[6],
    )


def solution(mesh):
    return jax.shard_map(
        body,
        mesh=mesh,
        in_specs=(
            P("dp", None, "ctx", None, None),
            P("dp", None, "ctx", None, None),
            P("dp"),
            P(),
            P(),
            P(None, "tensor", None),
            P("tensor", None),
            P(),
            P(),
            P(None, "tensor"),
            P("tensor"),
            P("tensor", None),
        ),
        out_specs=(
            P("dp", None, "ctx", None, None),
            P("dp", None, "ctx", None, None),
            P("tensor"),
            P("tensor"),
            P(None, "tensor", None),
            P("tensor", None),
            P("tensor"),
            P("tensor"),
            P(None, "tensor"),
            P("tensor"),
            P("tensor", None),
        ),
        check_vma=False,
    )
```

profile of v0, /device:TPU:0, one launch (start us, length us, event | category | flops | bytes accessed | tf_op | source)
XLA Modules:
  0.0 797.7 jit_solution(1816895675387504527)
XLA Ops:
  14.8 4.4 reshape.324
  27.1 81.0 %all-gather.2.cloned.1.call-done = bf16[8,2,8,64,512]{4,3,2,1,0:T(8,128)(2,1)} async-done(((bf16[8,2,1,64,512]{4,3,2,1,0:T(8,128)(2,1)}), bf16[8,2,8,64,512]{4,3,2,1,0:T(8,128)(2,1)}) %all-gather.2.cloned.1.call-update) | async-done | bytes 8388624 | tf_op jit(solution)/shard_map/all_gather | solution.py:64
  108.0 12.5 %reshape.326 = bf16[8,1024,4,128]{3,2,1,0:T(4,128)(2,1)} reshape(bf16[8,2,8,64,512]{4,3,2,1,0:T(8,128)(2,1)} %all-gather.2.cloned.1.call-done) | data formatting | bytes 16777216 | tf_op jit(solution)/shard_map/reshape | solution.py:67
  120.5 17.3 %fusion.48 = (bf16[8,1024,4,64]{3,2,1,0:T(4,128)(2,1)}, bf16[8,1024,4,64]{3,2,1,0:T(4,128)(2,1)}) fusion(bf16[8,1024,4,128]{3,2,1,0:T(4,128)(2,1)} %reshape.326), kind=kLoop, calls=%fused_computation.112 | loop fusion | bytes 16777216 | tf_op jit(solution)/shard_map/slice | solution.py:68
  137.9 12.8 %copy.61 = bf16[8,1024,4,64]{1,3,2,0:T(8,128)(2,1)} copy(bf16[8,1024,4,64]{3,2,1,0:T(4,128)(2,1)} %get-tuple-element.66) | data formatting | bytes 8388608
  150.6 12.7 %copy.60 = bf16[8,1024,4,64]{1,3,2,0:T(8,128)(2,1)} copy(bf16[8,1024,4,64]{3,2,1,0:T(4,128)(2,1)} %get-tuple-element.67) | data formatting | bytes 8388608
  163.4 5.2 fusion.49
  175.6 4.4 fusion.37
  183.0 10.7 %all-reduce.12.cloned.1.call-start = ((), (), s32[]{:S(2)}) async-start(), calls=%async_computation.2 | async-start | bytes 2097152 | tf_op jit(solution)/shard_map/psum | solution.py:116
  193.7 50.9 %all-reduce.10.cloned.1.call-done = f32[1024,512]{1,0:T(8,128)} async-done(((f32[1024,512]{1,0:T(8,128)}), f32[1024,512]{1,0:T(8,128)}) %all-reduce.10.cloned.1.call-update) | async-done | bytes 2097168 | tf_op jit(solution)/shard_map/psum | solution.py:92
  251.1 4.0 fusion.50
  258.9 40.1 %all-reduce.12.cloned.1.call-done = bf16[1024,512]{1,0:T(8,128)(2,1)} async-done(((bf16[1024,512]{1,0:T(8,128)(2,1)}), bf16[1024,512]{1,0:T(8,128)(2,1)}) %all-reduce.12.cloned.1.call-update) | async-done | bytes 1048592 | tf_op jit(solution)/shard_map/psum | solution.py:116
  307.9 12.3 %multiply_reduce_fusion = (f32[8,4,128]{2,1,0:T(4,128)S(1)}, f32[8,4,128,1024]{3,2,1,0:T(8,128)}) fusion(f32[8,4,128,1024]{3,2,1,0:T(8,128)} %copy-done.2, f32[8,4,128]{2,1,0:T(4,128)S(1)} %bitcast.110, bf16[8,128,4,64]{1,3,2,0:T(8,128)(2,1)S(1)} %copy.47, bf16[8,1024,4,64]{1,3,2,0:T(8,128)(2,1)} %copy.60), kind=kOutput, calls=%fused_computation.1 | convolution fusion | flops 549449728 | bytes 38305792 | tf_op jit(solution)/shard_map/cqhd,ckhd->chqk/dot_general | solution.py:132
  320.2 8.8 %convert_bitcast_fusion = bf16[8,1024,4,64]{1,3,2,0:T(8,128)(2,1)} fusion(bf16[8,128,4,64]{1,3,2,0:T(8,128)(2,1)S(1)} %copy.47, f32[8,4,128,1024]{3,2,1,0:T(8,128)} %copy-done.2, f32[8,4,128]{2,1,0:T(4,128)S(1)} %bitcast.111), kind=kOutput, calls=%fused_computation.23 | convolution fusion | flops 547356672 | bytes 21512192 | tf_op jit(solution)/shard_map/chqk,cqhd->ckhd/dot_general | solution.py:145
  328.9 11.8 %multiply_convert_fusion = bf16[8,4,128,1024]{3,2,1,0:T(8,128)(2,1)S(1)} fusion(f32[8,4,128,1024]{3,2,1,0:T(8,128)} %get-tuple-element.77, f32[8,4,128,1024]{3,2,1,0:T(8,128)} %copy-done.2, f32[8,4,128]{2,1,0:T(4,128)S(1)} %get-tuple-element.76, f32[8,4,128]{2,1,0:T(4,128)S(1)} %bitcast.112), kind=kLoop, calls=%fused_computation | loop fusion | flops 16777216 | bytes 41975808 | tf_op jit(solution)/shard_map/convert_element_type | solution.py:136
  347.2 8.3 %pad_maximum_fusion = bf16[8,1024,4,128]{1,3,2,0:T(8,128)(2,1)} fusion(bf16[8,1024,4,64]{1,3,2,0:T(8,128)(2,1)} %convert_bitcast_fusion, bf16[8,1024,4,64]{1,3,2,0:T(8,128)(2,1)} %fusion.13), kind=kLoop, calls=%fused_computation.9 | loop fusion | flops 16777216 | bytes 16777216 | tf_op jit(solution)/shard_map/concatenate | solution.py:151
  355.5 13.7 %copy.49 = bf16[8,1024,4,128]{3,2,1,0:T(4,128)(2,1)} copy(bf16[8,1024,4,128]{1,3,2,0:T(8,128)(2,1)} %pad_maximum_fusion) | data formatting | bytes 16777216 | tf_op jit(solution)/shard_map/concatenate | solution.py:151
  369.3 13.1 %convert_element_type.172 = bf16[8,2,8,64,512]{4,3,2,1,0:T(8,128)(2,1)} reshape(bf16[8,1024,4,128]{3,2,1,0:T(4,128)(2,1)} %copy.49) | data formatting | bytes 16777216 | tf_op jit(solution)/shard_map/convert_element_type | solution.py:154
  400.0 158.1 %all-reduce.14.cloned.1.call-done = bf16[8,2,8,64,512]{4,3,2,1,0:T(8,128)(2,1)} async-done(((bf16[8,2,8,64,512]{4,3,2,1,0:T(8,128)(2,1)}), bf16[8,2,8,64,512]{4,3,2,1,0:T(8,128)(2,1)}) %all-reduce.14.cloned.1.call-update) | async-done | bytes 8388624
  561.2 4.8 pad_maximum_fusion.1
  566.0 4.7 reshape.333
  584.8 96.2 %all-reduce.16.cloned.1.call-done = (bf16[512,4,192]{0,2,1:T(8,128)(2,1)}, bf16[256,512]{1,0:T(8,128)(2,1)}, bf16[512,1024]{1,0:T(8,128)(2,1)}, bf16[1024,512]{1,0:T(8,128)(2,1)}) async-done(((bf16[512,4,192]{0,2,1:T(8,128)(2,1)}, bf16[256,512]{1,0:T(8,128)(2,1)}, bf16[512,1024]{1,0:T(8,128)(2,1)}, bf16[1024,512]{1,0:T(8,128)(2,1)}), (bf16[512,4,192]{0,2,1:T(8,128)(2,1)}, bf16[256,512]{1,0:T(8,128)(2,1)}, ...) | async-done | bytes 3145744 | tf_op jit(solution)/shard_map/psum | solution.py:180
  687.7 58.0 %all-reduce.18.cloned.1.call-done = (bf16[1024,512]{1,0:T(8,128)(2,1)}, bf16[1024,512]{1,0:T(8,128)(2,1)}) async-done(((bf16[1024,512]{1,0:T(8,128)(2,1)}, bf16[1024,512]{1,0:T(8,128)(2,1)}), (bf16[1024,512]{1,0:T(8,128)(2,1)}, bf16[1024,512]{1,0:T(8,128)(2,1)})) %all-reduce.18.cloned.1.call-update) | async-done | bytes 2097168 | tf_op jit(solution)/shard_map/psum | solution.py:99
  749.4 33.2 %all-reduce.1 = (bf16[256]{0:T(256)(128)(2,1)S(1)}, bf16[256]{0:T(256)(128)(2,1)S(1)}, bf16[256]{0:T(256)(128)(2,1)S(1)}, bf16[256]{0:T(256)(128)(2,1)S(1)}, bf16[1024]{0:T(1024)(128)(2,1)S(1)}) all-reduce(bf16[256]{0:T(256)(128)(2,1)S(1)} %dynamic_slice.23, ...), channel_id=1, replica_groups=mesh['dp'=2,'ctx'=8,'tensor'=2] {'dp','ctx'}, use_global_device_ids=true, to_apply=%region_17.18 | all-reduce | flops 2048 | bytes 8192 | tf_op jit(solution)/shard_map/psum | solution.py:182
  (177 shorter events, 103.8 us)
Async XLA Ops:
  7.2 240.0 %copy-start = (bf16[512,1024]{1,0:T(8,128)(2,1)S(1)}, bf16[512,1024]{1,0:T(8,128)(2,1)}, u32[]{:S(2)}) copy-start(bf16[512,1024]{1,0:T(8,128)(2,1)} %param.21) | copy-start | bytes 3145732
  7.2 4.0 copy-start.5
  7.2 4.0 copy-start.29
  7.2 4.0 copy-start.33
  7.2 5.4 copy-start.37
  7.2 100.8 %all-gather.2.cloned.1.call-start = ((), (), s32[]{:S(2)}) async-start(), calls=%async_computation | async-start | bytes 9437184 | tf_op jit(solution)/shard_map/all_gather | solution.py:64
  23.1 221.5 %all-reduce.10.cloned.1.call-start = ((), (), s32[]{:S(2)}) async-start(), calls=%async_computation.1 | async-start | bytes 4194304 | tf_op jit(solution)/shard_map/psum | solution.py:92
  26.2 137.1 %copy-start.10 = (bf16[8,128,4,64]{1,3,2,0:T(8,128)(2,1)}, bf16[8,128,4,64]{1,3,2,0:T(8,128)(2,1)S(1)}, u32[]{:S(2)}) copy-start(bf16[8,128,4,64]{1,3,2,0:T(8,128)(2,1)S(1)} %copy.54) | copy-start | bytes 1572868
  168.6 7.1 copy-start.2
  168.6 7.1 copy-start.8
  175.6 5.6 copy-start.24
  183.0 116.0 %all-reduce.12.cloned.1.call-start = ((), (), s32[]{:S(2)}) async-start(), calls=%async_computation.2 | async-start | bytes 2097152 | tf_op jit(solution)/shard_map/psum | solution.py:116
  258.8 299.3 %all-reduce.14.cloned.1.call-start = ((), (), s32[]{:S(2)}) async-start(), calls=%async_computation.3 | async-start | bytes 16777216
  328.9 15.1 %copy-start.11 = (bf16[8,128,4,64]{1,3,2,0:T(8,128)(2,1)S(1)}, bf16[8,128,4,64]{1,3,2,0:T(8,128)(2,1)}, u32[]{:S(2)}) copy-start(bf16[8,128,4,64]{1,3,2,0:T(8,128)(2,1)} %copy-done.10) | copy-start | bytes 1572868
  382.4 298.6 %all-reduce.16.cloned.1.call-start = ((), (), s32[]{:S(2)}) async-start(), calls=%async_computation.4 | async-start | bytes 6291456 | tf_op jit(solution)/shard_map/psum | solution.py:180
  383.6 4.0 copy-start.43
  383.6 6.5 slice-start
  387.6 4.2 copy-start.4
  391.8 6.1 copy-start.18
  576.7 169.0 %all-reduce.18.cloned.1.call-start = ((), (), s32[]{:S(2)}) async-start(), calls=%async_computation.5 | async-start | bytes 4194304 | tf_op jit(solution)/shard_map/psum | solution.py:99
  577.9 4.0 copy-start.12
  577.9 4.0 copy-start.38
  685.5 60.2 %copy-start.6 = (bf16[8,2,1,64,512]{4,3,2,1,0:T(8,128)(2,1)S(1)}, bf16[8,2,1,64,512]{4,3,2,1,0:T(8,128)(2,1)}, u32[]{:S(2)}) copy-start(bf16[8,2,1,64,512]{4,3,2,1,0:T(8,128)(2,1)} %param.12) | copy-start | bytes 3145732
  685.5 60.2 %copy-start.30 = (f32[512]{0:T(512)S(1)}, f32[512]{0:T(512)}, u32[]{:S(2)}) copy-start(f32[512]{0:T(512)} %param.15) | copy-start | bytes 6148
  (28 other events, 52.2 us)
Sparse Core Ops, SparseCore 0:
  23.2 84.7 all-gather.1
  183.1 61.4 all-reduce.9
  258.9 40.0 all-reduce.11
  382.5 175.5 all-reduce.13
  576.8 104.1 all-reduce.15
  683.8 61.8 all-reduce.17
where the time goes:
time: 808 us; the launch traced here: 798 us
  waiting for transfers between devices  484 us (60%)
  local copies, waits for them, and re-layouts  126 us (16%)
  matrix products  69.8 us (9%)
  other arithmetic  57.9 us (7%)
  blocking collectives  33.2 us (4%)
  between operations  15 us (2%)
  starting transfers between devices  11.3 us (1%)
    unnamed x7, waiting for transfers between devices  158 us
    psum x1, waiting for transfers between devices, body(): lax.psum(grad_qkv.astype(jnp.bfloat16), ('dp', 'ctx')).astype(jnp.float32)  96.2 us
    all_gather x1, waiting for transfers between devices, body(): gathered = lax.all_gather(pairs, 'ctx', axis=2, tiled=True)  81 us
    psum x1, waiting for transfers between devices, body(): lax.psum(jnp.dot(activated_low, w_down, preferred_element_type=jnp.float3...  58 us
    psum x1, waiting for transfers between devices, body(): lax.psum(jnp.dot(mixed_flat, w_out, preferred_element_type=jnp.float32),...  50.9 us
    unnamed x96, local copies, waits for them, and re-layouts  43.7 us
    psum x1, waiting for transfers between devices, body(): lax.psum(jnp.einsum('rf,df->rd', grad_pre, w_up, preferred_element_type=j...  40.1 us
    psum x1, blocking collectives, body(): lax.psum(own_slice(grad_gain_attn).astype(jnp.bfloat16), ('dp', 'ctx'))  33.2 us
  transfers between devices with their start and end apart: 6, of which 6 were waited for; matrix products, arithmetic and copies ran while one was open for 4% of the time, Pallas kernels for 0%

commit v1 on v0

v1 whole, which is shorter than its diff:
```python
import functools

import jax
import jax.numpy as jnp
from jax import lax
from jax.experimental import pallas as pl
from jax.experimental.pallas import tpu as pltpu
from jax.sharding import PartitionSpec as P

PATCH = 64
EPSILON = 1e-05
MESH = pl.DeviceIdType.MESH
BF = jnp.bfloat16
F32 = jnp.float32

NN = (((1,), (0,)), ((), ()))
NT = (((1,), (1,)), ((), ()))
TN = (((0,), (0,)), ((), ()))


def dot(a, b, dims=NN):
    return lax.dot_general(a, b, dims, preferred_element_type=F32)


def bits_of(size):
    found, bit = [], 1
    while bit < size:
        found.append(bit)
        bit *= 2
    return found


def flip(index, bit):
    return index + bit - 2 * bit * ((index // bit) % 2)


def bit_of(index, bit):
    return (index // bit) % 2


def row_ds(start, size, unit=16):
    return pl.ds(pl.multiple_of(start, unit), size)


def remote(src, dst, send_sem, recv_sem, where):
    return pltpu.make_async_remote_copy(
        src_ref=src,
        dst_ref=dst,
        send_sem=send_sem,
        recv_sem=recv_sem,
        device_id=where,
        device_id_type=MESH,
    )


def arrived(dst, sem):
    pltpu.make_async_copy(dst, dst, sem).wait()


def norm_parts(values):
    mean = jnp.mean(values, axis=-1, keepdims=True)
    centered = values - mean
    var = jnp.mean(centered * centered, axis=-1, keepdims=True)
    rstd = lax.rsqrt(var + EPSILON)
    return centered * rstd, rstd


def norm_back(grad, gain, xhat, rstd):
    scaled = grad * gain
    first = jnp.mean(scaled, axis=-1, keepdims=True)
    second = jnp.mean(scaled * xhat, axis=-1, keepdims=True)
    return rstd * (scaled - first - xhat * second)


def plan_levels(lead, rows, order):
    levels = []
    for axis, bit in order:
        if axis == "tensor":
            lead //= 2
            kind = "t"
        elif rows % 32 == 0:
            rows //= 2
            kind = "r"
        else:
            kind = "f"
        levels.append((axis, bit, kind, lead, rows))
    return levels


class Reduce:
    def __init__(self, levels, acc, fin, bufs, ss, rs, place):
        self.levels, self.acc, self.fin = levels, acc, fin
        self.bufs, self.ss, self.rs, self.place = bufs, ss, rs, place
        self.lead, self.rows = acc.shape[0], acc.shape[1]
        self.toff, self.roff = 0, 0
        self.marks = []
        self.copy = None
        self.steps = []
        count = len(levels)
        for n in range(count):
            self.steps.append(functools.partial(self.step, n))
        self.steps.append(self.turn)

    def send(self, n):
        axis, bit, kind, lead, rows = self.levels[n]
        mine = bit_of(self.place[axis], bit)
        self.marks.append((self.toff, self.roff, self.lead, self.rows))
        toff, roff = self.toff, self.roff
        if kind == "t":
            toff = self.toff + (1 - mine) * lead
            self.toff = self.toff + mine * lead
        elif kind == "r":
            roff = self.roff + (1 - mine) * rows
            self.roff = self.roff + mine * rows
        self.lead, self.rows = lead, rows
        self.copy = remote(
            self.acc.at[pl.ds(toff, lead), row_ds(roff, rows)],
            self.bufs[n],
            self.ss.at[n],
            self.rs.at[n],
            {axis: flip(self.place[axis], bit)},
        )
        self.copy.start()

    def absorb(self, n):
        self.copy.wait()
        buf = self.bufs[n]
        part = 32 if self.rows % 32 == 0 else 16
        for a in range(self.lead):

            def add(b, _):
                off = pl.multiple_of(b * part, 16)
                at = row_ds(self.roff + off, part)
                old = self.acc[self.toff + a, at, :].astype(F32)
                new = buf[a, pl.ds(off, part), :].astype(F32)
                self.acc[self.toff + a, at, :] = (old + new).astype(BF)
                return 0

            lax.fori_loop(0, self.rows // part, add, 0)

    def step(self, n):
        if n > 0:
            self.absorb(n - 1)
        self.send(n)

    def turn(self):
        count = len(self.levels)
        self.absorb(count - 1)
        at = row_ds(self.roff, self.rows)
        self.fin[at, :] = self.acc[self.toff, at, :]
        back = [n for n in reversed(range(count)) if self.levels[n][2] == "r"]
        for k, n in enumerate(back):
            self.steps.append(functools.partial(self.gather, n, k == 0))
        self.steps.append(self.close)

    def gather(self, n, first):
        if not first:
            self.copy.wait()
        axis, bit, kind, lead, rows = self.levels[n]
        part = self.fin.at[row_ds(self.roff, rows)]
        count = len(self.levels)
        self.copy = remote(
            part,
            part,
            self.ss.at[count + n],
            self.rs.at[count + n],
            {axis: flip(self.place[axis], bit)},
        )
        self.copy.start()
        self.roff = self.marks[n][1]

    def close(self):
        self.copy.wait()

    def tick(self):
        if self.steps:
            self.steps.pop(0)()
            return True
        return False

    def drain(self):
        while self.tick():
            pass


def kernel(cfg, names, *refs):
    ref = dict(zip(names, refs))
    N, T, DP = cfg["N"], cfg["T"], cfg["DP"]
    L, R, FO, tok = cfg["L"], cfg["R"], cfg["FO"], cfg["tok"]
    D, HW, GW, G, FFh, QB = cfg["D"], cfg["HW"], cfg["GW"], cfg["G"], cfg["FFh"], cfg["QB"]
    head_dim = cfg["head_dim"]
    HG = GW // head_dim
    scale = head_dim ** (-0.5)
    d = lax.axis_index("dp")
    i = lax.axis_index("ctx")
    t = lax.axis_index("tensor")
    place = {"dp": d, "ctx": i, "tensor": t}
    x_in, cot_in = ref["x"], ref["cot"]
    sends = []

    bar = pltpu.get_barrier_semaphore()
    peers = [{"ctx": lax.rem(i + p, N)} for p in range(1, N)]
    peers += [{"tensor": lax.rem(t + p, T)} for p in range(1, T)]
    peers += [{"dp": flip(d, b)} for b in bits_of(DP)]
    for peer in peers:
        pl.semaphore_signal(bar, inc=1, device_id=peer, device_id_type=MESH)
    pl.semaphore_wait(bar, len(peers))

    frames = (i, 2 * N - 1 - i)

    def owns(h):
        return frames[h] // FO == t

    xb, rx, sx, fx = ref["xb"], ref["rx"], ref["sx"], ref["fx"]
    for p in range(N):
        c = lax.rem(i + p, N)
        for h in (0, 1):
            to = xb.at[row_ds(frames[h] * tok, tok)]

            @pl.when(owns(h))
            def _(p=p, c=c, h=h, to=to):
                if p == 0:
                    pltpu.make_async_copy(x_in.at[c, h], to, rx.at[frames[h]]).start()
                else:
                    remote(
                        x_in.at[c, h], to, sx.at[p, h], rx.at[frames[h]], {"ctx": c}
                    ).start()

            if p > 0:

                def done(p=p, c=c, h=h, to=to):
                    @pl.when(owns(h))
                    def _():
                        remote(
                            x_in.at[c, h], to, sx.at[p, h], rx.at[frames[h]], {"ctx": c}
                        ).wait_send()

                sends.append(done)

    def near(k):
        return t * FO + lax.rem(i + k, FO)

    for k in range(FO):
        f = near(k)
        part = xb.at[row_ds(f * tok, tok)]
        arrived(part, rx.at[f])
        for p in range(1, T):
            copy = remote(
                part, part, fx.at[p, k], rx.at[f], {"tensor": lax.rem(t + p, T)}
            )
            copy.start()
            sends.append(copy.wait_send)

    cb, rc, sc = ref["cb"], ref["rc"], ref["sc"]
    for p in range(N):
        c = lax.rem(i + p, N)
        for h in (0, 1):
            slot = lax.rem(frames[h], FO)
            to = cb.at[row_ds(slot * tok, tok)]

            @pl.when(owns(h))
            def _(p=p, c=c, h=h, to=to, slot=slot):
                if p == 0:
                    pltpu.make_async_copy(cot_in.at[c, h], to, rc.at[slot]).start()
                else:
                    remote(cot_in.at[c, h], to, sc.at[p, h], rc.at[slot], {"ctx": c}).start()

            if p > 0:

                def done(p=p, c=c, h=h, to=to, slot=slot):
                    @pl.when(owns(h))
                    def _():
                        remote(
                            cot_in.at[c, h], to, sc.at[p, h], rc.at[slot], {"ctx": c}
                        ).wait_send()

                sends.append(done)

    share = 2 * lax.rem(d, 2) + lax.rem(i, 2)
    wide = ("w_out", "w_up", "w_down")
    full = {n: ref[n + "_full"] for n in wide + ("bias",)}
    rw, sw, lw = ref["rw"], ref["sw"], ref["lw"]
    own_copies = []
    for n, name in enumerate(wide + ("bias",)):
        copy = pltpu.make_async_copy(ref[name], full[name].at[t], lw.at[n])
        copy.start()
        own_copies.append(copy)
    for p in range(1, T):
        to = {"tensor": lax.rem(t + p, T)}
        copy = remote(ref["bias"], full["bias"].at[t], sw.at[3, 0, p], rw.at[3, 0, t], to)
        copy.start()
        sends.append(copy.wait_send)
    for n, name in enumerate(wide):
        quarter = ref[name].shape[0] // 4
        at = row_ds(share * quarter, quarter)
        for p in range(1, T):
            to = {"tensor": lax.rem(t + p, T)}
            copy = remote(
                ref[name].at[at], full[name].at[t, at], sw.at[n, 0, p], rw.at[n, 0, t], to
            )
            copy.start()
            sends.append(copy.wait_send)

    other_dp = 2 * (1 - lax.rem(d, 2)) + lax.rem(i, 2)
    other_core = 2 * lax.rem(d, 2) + 1 - lax.rem(i, 2)
    other_both = 2 * (1 - lax.rem(d, 2)) + 1 - lax.rem(i, 2)

    def weight_part(name, s, which):
        quarter = ref[name].shape[0] // 4
        return full[name].at[s, row_ds(which * quarter, quarter)]

    def weights_second(n, name):
        for p in range(1, T):
            s = lax.rem(t + p, T)
            part = weight_part(name, s, share)
            arrived(part, rw.at[n, 0, s])
            for stage, to in ((1, {"dp": flip(d, 1)}), (2, {"ctx": flip(i, 1)})):
                copy = remote(part, part, sw.at[n, stage, p], rw.at[n, stage, s], to)
                copy.start()
                sends.append(copy.wait_send)

    def weights_third(n, name):
        for p in range(1, T):
            s = lax.rem(t + p, T)
            part = weight_part(name, s, other_dp)
            arrived(part, rw.at[n, 1, s])
            copy = remote(
                part, part, sw.at[n, 3, p], rw.at[n, 3, s], {"ctx": flip(i, 1)}
            )
            copy.start()
            sends.append(copy.wait_send)

    def weights_ready(n, name):
        own_copies[n].wait()
        for p in range(1, T):
            s = lax.rem(t + p, T)
            if name == "bias":
                arrived(full[name].at[s], rw.at[n, 0, s])
            else:
                arrived(weight_part(name, s, other_core), rw.at[n, 2, s])
                arrived(weight_part(name, s, other_both), rw.at[n, 3, s])

    RB = min(256, R)
    nb, qb_, kb_, vb_ = ref["nb"], ref["q"], ref["k"], ref["v"]
    vec = ref["vec"]
    wqkv = ref["w_qkv"]

    def project(start):
        rows = row_ds(start, RB, 64)
        xhat, _ = norm_parts(xb[rows, :].astype(F32))
        normed = (xhat * vec[0:1, :] + vec[1:2, :]).astype(BF)
        nb[rows, :] = normed
        packed = dot(normed, wqkv[...])
        for g in range(G):
            lo = g * GW
            qb_[g, rows, :] = (packed[:, lo : lo + GW].astype(BF).astype(F32) * scale).astype(BF)
            kb_[g, rows, :] = packed[:, HW + lo : HW + lo + GW].astype(BF)
            vb_[g, rows, :] = packed[:, 2 * HW + lo : 2 * HW + lo + GW].astype(BF)

    for k in range(R // RB):
        project(t * R + k * RB)
    for p in range(1, T):
        s = lax.rem(t + p, T)
        for k in range(FO):
            f = s * FO + k
            arrived(xb.at[row_ds(f * tok, tok)], rx.at[f])
        for k in range(R // RB):
            project(s * R + k * RB)

    for n, name in enumerate(wide):
        weights_second(n, name)

    live = ref["live"][i]
    probs, mo, mr = ref["probs"], ref["mo"], ref["mr"]
    rm, sm = ref["rm"], ref["sm"]
    piece = min(QB, R)
    NQ = L // QB
    lane = lax.broadcasted_iota(jnp.int32, (QB, GW), 1) // head_dim

    def pick(parts):
        out = parts[0]
        for a in range(1, HG):
            out = jnp.where(lane == a, parts[a], out)
        return out

    def only(values, a):
        if HG == 1:
            return values
        return jnp.where(lane == a, values, jnp.zeros_like(values))

    def hand_over(qb, g):
        for b in range(QB // piece):
            row = qb * QB + b * piece
            s = row // R
            slot = (row - s * R) // piece
            src = mo.at[pl.ds(row, piece), pl.ds(g * GW, GW)]
            dst = mr.at[t, pl.ds(row - s * R, piece), pl.ds(g * GW, GW)]
            index = row // piece

            @pl.when(s == t)
            def _():
                mr[t, pl.ds(row - s * R, piece), pl.ds(g * GW, GW)] = mo[
                    pl.ds(row, piece), pl.ds(g * GW, GW)
                ]

            @pl.when(s != t)
            def _():
                remote(src, dst, sm.at[index, g], rm.at[t, slot, g], {"tensor": s}).start()

            def done(s=s, src=src, dst=dst, index=index, slot=slot):
                @pl.when(s != t)
                def _():
                    remote(
                        src, dst, sm.at[index, g], rm.at[t, slot, g], {"tensor": s}
                    ).wait_send()

            sends.append(done)

    pumps = [functools.partial(weights_third, n, name) for n, name in enumerate(wide)]
    for qb in reversed(range(NQ)):
        K = (qb + 1) * QB
        rows = pl.ds(qb * QB, QB)
        row_frame = (qb * QB + lax.broadcasted_iota(jnp.int32, (QB, K), 0)) // PATCH
        col_frame = lax.broadcasted_iota(jnp.int32, (QB, K), 1) // PATCH
        allowed = (col_frame <= row_frame) & (col_frame < live)
        shift = jnp.where(allowed, 0.0, -1e30)
        for g in range(G):
            qv = qb_[g, rows, :]
            kv = kb_[g, pl.ds(0, K), :]
            vv = vb_[g, pl.ds(0, K), :]
            outs = []
            for a in range(HG):
                scores = dot(only(qv, a), kv, NT) + shift
                top = jnp.max(scores, axis=-1, keepdims=True)
                weights = jnp.exp(scores - top)
                total = jnp.sum(weights, axis=-1, keepdims=True)
                prob = (weights * (1.0 / total)).astype(BF)
                probs[g * HG + a, rows, pl.ds(0, K)] = prob
                outs.append(dot(prob, vv))
            mo[rows, pl.ds(g * GW, GW)] = pick(outs).astype(BF)
            hand_over(qb, g)
        if pumps:
            pumps.pop(0)()
    while pumps:
        pumps.pop(0)()

    for n, name in enumerate(wide + ("bias",)):
        weights_ready(n, name)
    for p in range(1, T):
        s = lax.rem(t + p, T)
        for slot in range(R // piece):
            for g in range(G):
                arrived(
                    mr.at[s, pl.ds(slot * piece, piece), pl.ds(g * GW, GW)], rm.at[s, slot, g]
                )
    for k in range(FO):
        arrived(cb.at[pl.ds(k * tok, tok)], rc.at[k])

    wof, wuf, wdf, bf_ = full["w_out"], full["w_up"], full["w_down"], full["bias"]
    second, act, gpre = ref["second"], ref["act"], ref["gpre"]
    mlow, gmid, gst, gx = ref["mlow"], ref["gmid"], ref["gst"], ref["gx"]
    ob, out_ref, ig_ref = ref["ob"], ref["out"], ref["ig"]
    sv = ref["sv"]
    mlp_sum, sec_sum = ref["mlp_sum"], ref["sec_sum"]
    RC = min(256, R)
    FT = min(512, FFh)
    c0 = 0.7978845608028654
    sv[0] = jnp.zeros_like(sv[0])

    def frame_home(k):
        f = t * FO + k
        high = f // N
        j = f * (1 - high) + (2 * N - 1 - f) * high
        return j, high

    def give_back(buf, dst_ref, ss, rs, k):
        j, h = frame_home(k)
        src = buf.at[pl.ds(k * tok, tok)]

        @pl.when(j == i)
        def _():
            pltpu.make_async_copy(src, dst_ref.at[i, h], rs.at[i, h]).start()

        @pl.when(j != i)
        def _():
            remote(src, dst_ref.at[i, h], ss.at[k], rs.at[i, h], {"ctx": j}).start()

        def done():
            @pl.when(j != i)
            def _():
                remote(src, dst_ref.at[i, h], ss.at[k], rs.at[i, h], {"ctx": j}).wait_send()

        sends.append(done)

    def pass_on(dst_ref, fs, rs):
        for p in range(N):
            c = lax.rem(i + p, N)
            for h in (0, 1):
                part = dst_ref.at[c, h]

                @pl.when(owns(h))
                def _(p=p, c=c, h=h, part=part):
                    arrived(part, rs.at[c, h])
                    for q in range(1, T):
                        remote(
                            part, part, fs.at[q, p, h], rs.at[c, h], {"tensor": lax.rem(t + q, T)}
                        ).start()

                def done(p=p, c=c, h=h, part=part):
                    @pl.when(owns(h))
                    def _():
                        for q in range(1, T):
                            remote(
                                part,
                                part,
                                fs.at[q, p, h],
                                rs.at[c, h],
                                {"tensor": lax.rem(t + q, T)},
                            ).wait_send()

                sends.append(done)

    def take_rest(dst_ref, rs):
        for c in range(N):
            for h in (0, 1):

                @pl.when(frames[h] // FO != t)
                def _(c=c, h=h):
                    arrived(dst_ref.at[c, h], rs.at[c, h])

    sg, rg = ref["sg"], ref["rg"]
    for rc_index in range(R // RC):
        rows = pl.ds(rc_index * RC, RC)
        attn = dot(mr[0, rows, :], wof[0])
        for s in range(1, T):
            attn = attn + dot(mr[s, rows, :], wof[s])
        middle = xb[row_ds(t * R + rc_index * RC, RC, 64), :].astype(F32) + attn
        xhat, rstd = norm_parts(middle)
        sec = (xhat * vec[2:3, :] + vec[3:4, :]).astype(BF)
        second[rows, :] = sec
        cot = cb[rows, :]
        for s in range(T):
            for j in range(FFh // FT):
                cols = pl.ds(j * FT, FT)
                pre = dot(sec, wuf[s, :, cols]) + bf_[s, 0:1, cols]
                gact = dot(cot, wdf[s, cols, :], NT)
                sq = pre * pre
                th = jnp.tanh(c0 * pre * (1.0 + 0.044715 * sq))
                half = 0.5 * (1.0 + th)
                a = (pre * half).astype(BF)
                slope = half + 0.5 * pre * (1.0 - th * th) * (c0 * (1.0 + 0.134145 * sq))
                gp = (gact * slope).astype(BF)
                act[s, rows, cols] = a
                gpre[s, rows, cols] = gp
                sv[0, 4 + s : 5 + s, cols] = sv[0, 4 + s : 5 + s, cols] + jnp.sum(
                    gp.astype(F32), axis=0, keepdims=True
                )
                up = dot(a, wdf[s, cols, :])
                back = dot(gp, wuf[s, :, cols], NT)
                if s == 0 and j == 0:
                    mlp_sum[...] = up
                    sec_sum[...] = back
                else:
                    mlp_sum[...] = mlp_sum[...] + up
                    sec_sum[...] = sec_sum[...] + back
        ob[rows, :] = (middle + mlp_sum[...]).astype(BF)
        gsec = sec_sum[...]
        sv[0, 2:3, 0:D] = sv[0, 2:3, 0:D] + jnp.sum(gsec * xhat, axis=0, keepdims=True)
        sv[0, 3:4, 0:D] = sv[0, 3:4, 0:D] + jnp.sum(gsec, axis=0, keepdims=True)
        gm = cot.astype(F32) + norm_back(gsec, vec[2:3, :], xhat, rstd)
        gmid[rows, :] = gm
        low = gm.astype(BF)
        mlow[rows, :] = low
        for s in range(T):
            gst[s, rows, :] = dot(low, wof[s], NT).astype(BF)
            src = gst.at[s, rows]
            dst = gx.at[row_ds(t * R + rc_index * RC, RC, 64)]

            @pl.when(s == t)
            def _():
                gx[row_ds(t * R + rc_index * RC, RC, 64), :] = gst[s, rows, :]

            @pl.when(s != t)
            def _():
                remote(
                    src, dst, sg.at[s, rc_index], rg.at[t, rc_index], {"tensor": s}
                ).start()

            def done(s=s, src=src, dst=dst, rc_index=rc_index):
                @pl.when(s != t)
                def _():
                    remote(
                        src, dst, sg.at[s, rc_index], rg.at[t, rc_index], {"tensor": s}
                    ).wait_send()

            sends.append(done)
        for k in range(rc_index * RC // tok, (rc_index + 1) * RC // tok):
            give_back(ob, out_ref, ref["so"], ref["ro"], k)

    reduces = {}
    for name in cfg["plans"]:
        levels = cfg["plans"][name]
        bufs = [ref[f"{name}_buf{n}"] for n in range(len(levels))]
        reduces[name] = Reduce(
            levels, ref[name + "_acc"], ref[name + "_fin"], bufs, ref[name + "_ss"],
            ref[name + "_rs"], place,
        )
    cot = cb[...]
    for s in range(T):
        ref["down_acc"][s] = dot(act[s], cot, TN).astype(BF)
    reduces["down"].tick()
    for s in range(T):
        ref["up_acc"][s] = dot(second[...], gpre[s], TN).astype(BF)
    reduces["up"].tick()
    for s in range(T):
        ref["out_acc"][s] = dot(mr[s], mlow[...], TN).astype(BF)
    reduces["out"].tick()

    for p in range(1, T):
        s = lax.rem(t + p, T)
        for n in range(R // RC):
            arrived(gx.at[row_ds(s * R + n * RC, RC, 64)], rg.at[s, n])

    dk, dv, gpb = ref["dk"], ref["dv"], ref["gpb"]
    turns = 0
    for g in range(G):
        for qb in reversed(range(NQ)):
            K = (qb + 1) * QB
            rows = pl.ds(qb * QB, QB)
            keys = pl.ds(0, K)
            lanes = pl.ds(g * GW, GW)
            go = gx[rows, lanes]
            prod = go.astype(F32) * mo[rows, lanes].astype(F32)
            qv = qb_[g, rows, :]
            kv = kb_[g, keys, :]
            vv = vb_[g, keys, :]
            outs = []
            dk_sum = dv_sum = None
            for a in range(HG):
                delta = jnp.sum(only(prod, a), axis=-1, keepdims=True)
                goa = only(go, a)
                prob = probs[g * HG + a, rows, keys]
                gprob = dot(goa, vv, NT)
                gs = (prob.astype(F32) * (gprob - delta)).astype(BF)
                outs.append(dot(gs, kv))
                dk_part = dot(gs, only(qv, a), TN)
                dv_part = dot(prob, goa, TN)
                dk_sum = dk_part if dk_sum is None else dk_sum + dk_part
                dv_sum = dv_part if dv_sum is None else dv_sum + dv_part
            gpb[rows, lanes] = (pick(outs) * scale).astype(BF)
            if qb == NQ - 1:
                dk[keys, :] = dk_sum
                dv[keys, :] = dv_sum
            else:
                dk[keys, :] = dk[keys, :] + dk_sum
                dv[keys, :] = dv[keys, :] + dv_sum
            if turns == 1:
                pass_on(out_ref, ref["fo"], ref["ro"])
            reduces["down"].tick()
            reduces["up"].tick()
            reduces["out"].tick()
            turns += 1
        gpb[:, pl.ds(HW + g * GW, GW)] = dk[...].astype(BF)
        gpb[:, pl.ds(2 * HW + g * GW, GW)] = dv[...].astype(BF)

    gns, gnr = ref["gns"], ref["gnr"]
    for p in range(1, T):
        s = lax.rem(t + p, T)
        gns[p - 1] = dot(gpb[row_ds(s * R, R, 64), :], wqkv[...], NT).astype(BF)
        copy = remote(gns.at[p - 1], gnr.at[p - 1], ref["sn"].at[p - 1], ref["rn"].at[p - 1], {"tensor": s})
        copy.start()
        sends.append(copy.wait_send)
    ref["qkv_acc"][0] = dot(nb[...], gpb[...], TN).astype(BF)
    reduces["qkv"].tick()
    own = dot(gpb[row_ds(t * R, R, 64), :], wqkv[...], NT)
    for p in range(1, T):
        arrived(gnr.at[p - 1], ref["rn"].at[p - 1])
        own = own + gnr[p - 1].astype(F32)
    xhat, rstd = norm_parts(xb[row_ds(t * R, R, 64), :].astype(F32))
    sv[0, 0:1, 0:D] = jnp.sum(own * xhat, axis=0, keepdims=True)
    sv[0, 1:2, 0:D] = jnp.sum(own, axis=0, keepdims=True)
    igb = ref["igb"]
    igb[...] = (gmid[...] + norm_back(own, vec[0:1, :], xhat, rstd)).astype(BF)
    for k in range(FO):
        give_back(igb, ig_ref, ref["si"], ref["ri"], k)

    rsv = ref["rsv"]
    everyone = [(a, b) for a, n in (("ctx", N), ("dp", DP), ("tensor", T)) for b in bits_of(n)]
    for n, (axis, bit) in enumerate(everyone):
        copy = remote(
            sv.at[n], rsv.at[n], ref["sv_ss"].at[n], ref["sv_rs"].at[n],
            {axis: flip(place[axis], bit)},
        )
        copy.start()
        reduces["qkv"].tick()
        copy.wait()
        sv[n + 1] = sv[n] + rsv[n]
    pass_on(ig_ref, ref["fi"], ref["ri"])
    last = sv[len(everyone)]
    part = D // T
    gains = last[0:4, 0:part]
    bias = last[4:5, 0:FFh]
    for s in range(1, T):
        gains = jnp.where(t == s, last[0:4, s * part : (s + 1) * part], gains)
        bias = jnp.where(t == s, last[4 + s : 5 + s, 0:FFh], bias)
    ref["gains"][...] = gains
    ref["bias_out"][...] = bias

    for name in ("down", "up", "out", "qkv"):
        reduces[name].drain()
    take_rest(out_ref, ref["ro"])
    take_rest(ig_ref, ref["ri"])
    for done in sends:
        done()


def body(
    sizes,
    inputs,
    cotangent,
    live_frames,
    gain_attn,
    shift_attn,
    w_qkv,
    w_out,
    gain_mlp,
    shift_mlp,
    w_up,
    up_bias,
    w_down,
):
    N, T, DP = sizes["ctx"], sizes["tensor"], sizes["dp"]
    C, _, _, tok, D = inputs.shape
    heads, head_dim = w_qkv.shape[1], w_qkv.shape[2] // 3
    HW = heads * head_dim
    GW = min(128, HW)
    FFh = w_up.shape[1]
    L = 2 * N * tok
    R = L // T
    cfg = dict(
        N=N, T=T, DP=DP, L=L, R=R, FO=2 * N // T, tok=tok, D=D, HW=HW, GW=GW, G=HW // GW,
        FFh=FFh, QB=256, head_dim=head_dim,
    )
    G = cfg["G"]
    core, rest = [("ctx", 1)], [("ctx", b) for b in bits_of(N)[1:]]
    over_dp = [("dp", b) for b in bits_of(DP)]
    over_t = [("tensor", b) for b in reversed(bits_of(T))]
    cfg["plans"] = plans = {
        "down": plan_levels(T, FFh, core + over_dp + over_t + rest),
        "up": plan_levels(T, D, core + over_t + over_dp + rest),
        "out": plan_levels(T, HW, core + over_t + over_dp + rest),
        "qkv": plan_levels(1, D, core + over_dp + rest),
    }
    widths = {"down": D, "up": FFh, "out": D, "qkv": 3 * HW}
    leads = {"down": (T, FFh), "up": (T, D), "out": (T, HW), "qkv": (1, D)}

    x = inputs.reshape(C, 2, tok, D)
    cot = cotangent.reshape(C, 2, tok, D)
    wq = w_qkv.reshape(D, heads, 3, head_dim).transpose(0, 2, 1, 3).reshape(D, 3 * HW)
    vec = jnp.stack([gain_attn, shift_attn, gain_mlp, shift_mlp] * 2)
    bias = jnp.broadcast_to(up_bias[None], (8, FFh))

    vm = pl.BlockSpec(memory_space=pltpu.VMEM)
    hbm = pl.BlockSpec(memory_space=pl.ANY)
    ins = [
        ("x", x, hbm),
        ("cot", cot, hbm),
        ("live", live_frames, pl.BlockSpec(memory_space=pltpu.SMEM)),
        ("vec", vec, vm),
        ("w_qkv", wq, vm),
        ("w_out", w_out, hbm),
        ("w_up", w_up, hbm),
        ("w_down", w_down, hbm),
        ("bias", bias, vm),
    ]
    S = jax.ShapeDtypeStruct
    outs = [
        ("out", S((C, 2, tok, D), BF)),
        ("ig", S((C, 2, tok, D), BF)),
        ("down_fin", S((FFh, D), BF)),
        ("up_fin", S((D, FFh), BF)),
        ("out_fin", S((HW, D), BF)),
        ("qkv_fin", S((D, 3 * HW), BF)),
        ("gains", S((4, D // T), F32)),
        ("bias_out", S((1, FFh), F32)),
    ]
    W = max(D, FFh)
    SR = -(-(4 + T) // 8) * 8
    n_all = len(bits_of(N)) + len(bits_of(DP)) + len(bits_of(T))
    RC = min(256, R)
    piece = min(cfg["QB"], R)
    FO = cfg["FO"]
    dma = pltpu.SemaphoreType.DMA
    V = pltpu.VMEM
    scratch = dict(
        xb=V((L, D), BF), rx=dma((2 * N,)), sx=dma((N, 2)), fx=dma((T, FO)),
        cb=V((R, D), BF), rc=dma((FO,)), sc=dma((N, 2)),
        w_out_full=V((T, HW, D), BF), w_up_full=V((T, D, FFh), BF),
        w_down_full=V((T, FFh, D), BF), bias_full=V((T, 8, FFh), F32),
        rw=dma((4, 4, T)), sw=dma((4, 4, T)), lw=dma((4,)),
        nb=V((L, D), BF), q=V((G, L, GW), BF), k=V((G, L, GW), BF), v=V((G, L, GW), BF),
        probs=V((heads, L, L), BF), mo=V((L, HW), BF), mr=V((T, R, HW), BF),
        rm=dma((T, R // piece, G)), sm=dma((L // piece, G)),
        second=V((R, D), BF), act=V((T, R, FFh), BF), gpre=V((T, R, FFh), BF),
        mlow=V((R, D), BF), gmid=V((R, D), F32), gst=V((T, R, HW), BF), gx=V((L, HW), BF),
        sg=dma((T, R // RC)), rg=dma((T, R // RC)),
        ob=V((R, D), BF), so=dma((FO,)), ro=dma((N, 2)), fo=dma((T, N, 2)),
        igb=V((R, D), BF), si=dma((FO,)), ri=dma((N, 2)), fi=dma((T, N, 2)),
        mlp_sum=V((RC, D), F32), sec_sum=V((RC, D), F32),
        sv=V((n_all + 1, SR, W), F32), rsv=V((n_all, SR, W), F32),
        sv_ss=dma((n_all,)), sv_rs=dma((n_all,)),
        dk=V((L, GW), F32), dv=V((L, GW), F32), gpb=V((L, 3 * HW), BF),
        gns=V((max(T - 1, 1), R, D), BF), gnr=V((max(T - 1, 1), R, D), BF),
        sn=dma((T,)), rn=dma((T,)),
    )
    for name, levels in plans.items():
        scratch[name + "_acc"] = V(leads[name] + (widths[name],), BF)
        scratch[name + "_ss"] = dma((2 * len(levels),))
        scratch[name + "_rs"] = dma((2 * len(levels),))
        for n, (_, _, _, lead, rows) in enumerate(levels):
            scratch[f"{name}_buf{n}"] = V((lead, rows, widths[name]), BF)
    names = [n for n, *_ in ins] + [n for n, _ in outs] + list(scratch)
    results = pl.pallas_call(
        functools.partial(kernel, cfg, names),
        out_shape=[s for _, s in outs],
        in_specs=[s for _, _, s in ins],
        out_specs=[vm] * len(outs),
        scratch_shapes=list(scratch.values()),
        compiler_params=pltpu.CompilerParams(
            collective_id=0, has_side_effects=True, vmem_limit_bytes=60 * 2**20
        ),
    )(*[a for _, a, _ in ins])
    got = dict(zip([n for n, _ in outs], results))
    grad_qkv = (
        got["qkv_fin"]
        .reshape(D, 3, heads, head_dim)
        .transpose(0, 2, 1, 3)
        .reshape(w_qkv.shape)
        .astype(F32)
    )
    gains = got["gains"]
    return (
        got["out"].reshape(inputs.shape),
        got["ig"].reshape(inputs.shape),
        gains[0],
        gains[1],
        grad_qkv,
        got["out_fin"].astype(F32),
        gains[2],
        gains[3],
        got["up_fin"].astype(F32),
        got["bias_out"][0],
        got["down_fin"].astype(F32),
    )


def solution(mesh):
    return jax.shard_map(
        functools.partial(body, dict(mesh.shape)),
        mesh=mesh,
        in_specs=(
            P("dp", None, "ctx", None, None),
            P("dp", None, "ctx", None, None),
            P("dp"),
            P(),
            P(),
            P(None, "tensor", None),
            P("tensor", None),
            P(),
            P(),
            P(None, "tensor"),
            P("tensor"),
            P("tensor", None),
        ),
        out_specs=(
            P("dp", None, "ctx", None, None),
            P("dp", None, "ctx", None, None),
            P("tensor"),
            P("tensor"),
            P(None, "tensor", None),
            P("tensor", None),
            P("tensor"),
            P("tensor"),
            P(None, "tensor"),
            P("tensor"),
            P("tensor", None),
        ),
        check_vma=False,
    )
```

time: 808 us -> 201 us (0.25); the launches traced: 798 us -> 199 us
  waiting for transfers between devices: 484 us -> 0 us
  Pallas kernels: 0 us -> 184 us
  local copies, waits for them, and re-layouts: 126 us -> 10.4 us
  matrix products: 69.8 us -> 0 us
  other arithmetic: 57.9 us -> 4.03 us
  blocking collectives: 33.2 us -> 0 us
  between operations: 15 us -> 0.73 us
  starting transfers between devices: 11.3 us -> 0 us
    psum x4 -> x0, waiting for transfers between devices: 245 us -> none  [the longest x1 96.2 us: body(): lax.psum(grad_qkv.astype(jnp.bfloat16), ('dp', 'ctx')).astype(jnp.float32)]
    pallas_call x0 -> x1, Pallas kernels: none -> 184 us  [body(): pl.pallas_call(functools.partial(kernel, cfg, names), out_shape=[s for _,...]
    unnamed x7 -> x0, waiting for transfers between devices: 158 us -> none
    all_gather x1 -> x0, waiting for transfers between devices: 81 us -> none  [body(): gathered = lax.all_gather(pairs, 'ctx', axis=2, tiled=True)]
    dot_general x18 -> x0, matrix products: 69.8 us -> none  [the longest x1 12.3 us: body(): jnp.einsum('cqhd,ckhd->chqk', grad_mixed, value_part, preferred_element_t...]
    unnamed x96 -> x25, local copies, waits for them, and re-layouts: 43.7 us -> 2.62 us
    psum x1 -> x0, blocking collectives: 33.2 us -> none  [body(): lax.psum(own_slice(grad_gain_attn).astype(jnp.bfloat16), ('dp', 'ctx'))]
    reshape x8 -> x1, local copies, waits for them, and re-layouts: 30.5 us -> 1.16 us  [body(): w_qkv.reshape(D, heads, 3, head_dim).transpose(0, 2, 1, 3)]
  transfers between devices with their start and end apart: 6 -> 0, of which waited for: 6 -> 0; matrix products, arithmetic and copies ran while one was open for 4% -> 0% of each run, Pallas kernels for 0% -> 0%
where the time goes in v1:
time: 201 us; the launch traced here: 199 us
  Pallas kernels  184 us (92%)
  local copies, waits for them, and re-layouts  10.4 us (5%)
  other arithmetic  4.03 us (2%)
    pallas_call x1, Pallas kernels, body(): pl.pallas_call(functools.partial(kernel, cfg, names), out_shape=[s for _,...  184 us

profile of v1, /device:TPU:0, one launch (start us, length us, event | category | flops | bytes accessed | tf_op | source)
XLA Modules:
  0.0 199.5 jit_solution(10899588005073416686)
XLA Ops:
  0.6 0.0 copy-start.9
  0.7 0.0 copy-start.5
  0.7 0.0 copy-start.6
  0.7 0.0 copy-start.7
  0.7 0.0 copy-start.8
  0.7 1.2 copy.31
  1.9 1.2 copy.32.refs_4_
  3.1 0.0 copy-done.9
  3.1 0.6 broadcast_in_dim.2.refs_8_
  3.7 0.0 copy-done.5
  3.7 0.0 copy-done.6
  3.7 0.0 copy-done.8
  3.7 0.6 stack.23.refs_3_
  4.4 184.2 %shard_map.203 = (bf16[8,2,64,512]{3,2,1,0:T(8,128)(2,1)}, bf16[8,2,64,512]{3,2,1,0:T(8,128)(2,1)}, bf16[1024,512]{1,0:T(8,128)(2,1)}, bf16[512,1024]{1,0:T(8,12...) custom-call(bf16[8,2,64,512]{3,2,1,0:T(8,128)(2,1)} %bitcast.30, ...), custom_call_target="tpu_custom_call" | custom-call | tf_op jit(solution)/shard_map/pallas_call | solution.py:823
  188.6 1.4 fusion
  190.0 1.4 copy.33
  191.5 1.4 copy.34
  192.8 0.0 copy-done.1
  192.9 1.6 convert_element_type.26
  194.4 1.6 convert_element_type.27
  196.1 0.9 convert_element_type.25
  196.9 1.0 copy.40
  197.9 1.0 copy.41
  198.9 0.6 copy.42
  (12 shorter events, 0.0 us)
Async XLA Ops:
  0.6 2.5 %copy-start.9 = (f32[1024]{0:T(1024)S(1)}, f32[1024]{0:T(1024)}, u32[]{:S(2)}) copy-start(f32[1024]{0:T(1024)} %param.22) | copy-start | bytes 12292
  0.7 3.1 %copy-start.5 = (f32[512]{0:T(512)S(1)}, f32[512]{0:T(512)}, u32[]{:S(2)}) copy-start(f32[512]{0:T(512)} %param.15) | copy-start | bytes 6148
  0.7 3.1 %copy-start.6 = (f32[512]{0:T(512)S(1)}, f32[512]{0:T(512)}, u32[]{:S(2)}) copy-start(f32[512]{0:T(512)} %param.16) | copy-start | bytes 6148
  0.7 3.0 %copy-start.7 = (f32[512]{0:T(512)S(1)}, f32[512]{0:T(512)}, u32[]{:S(2)}) copy-start(f32[512]{0:T(512)} %param.19) | copy-start | bytes 6148
  0.7 3.0 %copy-start.8 = (f32[512]{0:T(512)S(1)}, f32[512]{0:T(512)}, u32[]{:S(2)}) copy-start(f32[512]{0:T(512)} %param.20) | copy-start | bytes 6148
  191.5 1.4 copy-start.1
  192.8 1.6 copy-start
  194.4 1.6 copy-start.4
  194.4 2.5 %copy-start.3 = (bf16[8,2,64,512]{3,2,1,0:T(8,128)(2,1)S(1)}, bf16[8,2,64,512]{3,2,1,0:T(8,128)(2,1)}, u32[]{:S(2)}) copy-start(bf16[8,2,64,512]{3,2,1,0:T(8,128)(2,1)} %get-tuple-element.19) | copy-start | bytes 3145732
  196.1 1.8 copy-start.2
  196.9 1.9 copy-start.10

commit v2 on v1

--- a/solution.py
+++ b/solution.py
@@ -1,4 +1,5 @@
 import functools
+from types import SimpleNamespace
 
 import jax
 import jax.numpy as jnp
@@ -74,8 +75,11 @@
 
 def plan_levels(lead, rows, order):
     levels = []
-    for axis, bit in order:
-        if axis == "tensor":
+    for axis, bit, *forced in order:
+        if forced:
+            kind = forced[0]
+            rows = rows // 2 if kind == "p" else rows
+        elif axis == "tensor":
             lead //= 2
             kind = "t"
         elif rows % 32 == 0:
@@ -85,6 +89,25 @@
             kind = "f"
         levels.append((axis, bit, kind, lead, rows))
     return levels
+
+
+ORDERS = {
+    "down0": "yxzZ",
+    "down1": "xzyZ",
+    "up0": "zyxZ",
+    "up1": "yxzZ",
+    "out": "xyzR",
+    "qkv0": "yxzZ",
+    "qkv1": "xyzZ",
+}
+CHUNKS = tuple(ORDERS)
+VECTORS, OUTPUT, INPUT_GRAD, MARK = range(7, 11)
+ORDER = tuple(CHUNKS[n] for n in (2, 3, 0, 1))
+SCRIPT = (
+    10, 3, 2, 0, 1, 4, 10, 10, 10, 8, 10, 8, 5, 10, 10, 8, 10, 3, 10, 8, 1, 6, 10, 4, 2, 7, 0,
+    3, 1, 6, 9, 0, 9, 5, 7, 9, 3, 9, 0, 5, 7, 4, 3, 5, 7, 2, 4, 0, 1, 3, 6, 5, 2, 4, 0, 6, 1, 3,
+    5, 3, 2, 0, 4, 1, 0, 5, 6, 4, 5, 2, 7, 6, 1, 1, 4, 4, 2, 2, 6, 6,
+)
 
 
 class Reduce:
@@ -106,6 +129,18 @@
         mine = bit_of(self.place[axis], bit)
         self.marks.append((self.toff, self.roff, self.lead, self.rows))
         toff, roff = self.toff, self.roff
+        dst = self.bufs[n]
+        if kind == "p":
+            toff = mine
+            roff = self.roff + (1 - mine) * rows
+            self.roff = self.roff + mine * rows
+            dst = self.acc.at[pl.ds(toff, 1), row_ds(roff, rows)]
+            self.copy = remote(
+                dst, dst, self.ss.at[n], self.rs.at[n], {axis: flip(self.place[axis], bit)}
+            )
+            self.lead, self.rows = lead, rows
+            self.copy.start()
+            return
         if kind == "t":
             toff = self.toff + (1 - mine) * lead
             self.toff = self.toff + mine * lead
@@ -115,7 +150,7 @@
         self.lead, self.rows = lead, rows
         self.copy = remote(
             self.acc.at[pl.ds(toff, lead), row_ds(roff, rows)],
-            self.bufs[n],
+            dst,
             self.ss.at[n],
             self.rs.at[n],
             {axis: flip(self.place[axis], bit)},
@@ -124,6 +159,8 @@
 
     def absorb(self, n):
         self.copy.wait()
+        if self.levels[n][2] == "p":
+            return
         buf = self.bufs[n]
         part = 32 if self.rows % 32 == 0 else 16
         for a in range(self.lead):
@@ -148,9 +185,12 @@
         self.absorb(count - 1)
         at = row_ds(self.roff, self.rows)
         self.fin[at, :] = self.acc[self.toff, at, :]
-        back = [n for n in reversed(range(count)) if self.levels[n][2] == "r"]
+        back = [n for n in reversed(range(count)) if self.levels[n][2] in "pr"]
         for k, n in enumerate(back):
-            self.steps.append(functools.partial(self.gather, n, k == 0))
+            if k == 0:
+                self.gather(n, True)
+            else:
+                self.steps.append(functools.partial(self.gather, n, False))
         self.steps.append(self.close)
 
     def gather(self, n, first):
@@ -183,19 +223,19 @@
             pass
 
 
-def kernel(cfg, names, *refs):
-    ref = dict(zip(names, refs))
-    N, T, DP = cfg["N"], cfg["T"], cfg["DP"]
-    L, R, FO, tok = cfg["L"], cfg["R"], cfg["FO"], cfg["tok"]
-    D, HW, GW, G, FFh, QB = cfg["D"], cfg["HW"], cfg["GW"], cfg["G"], cfg["FFh"], cfg["QB"]
-    head_dim = cfg["head_dim"]
+def spread_kernel(cfg, names, *refs):
+    ref = SimpleNamespace(**dict(zip(names, refs)))
+    N, T, DP = cfg.N, cfg.T, cfg.DP
+    L, R, FO, tok = cfg.L, cfg.R, cfg.FO, cfg.tok
+    D, HW, GW, G, FFh, QB = cfg.D, cfg.HW, cfg.GW, cfg.G, cfg.FFh, cfg.QB
+    head_dim = cfg.head_dim
     HG = GW // head_dim
     scale = head_dim ** (-0.5)
     d = lax.axis_index("dp")
     i = lax.axis_index("ctx")
     t = lax.axis_index("tensor")
     place = {"dp": d, "ctx": i, "tensor": t}
-    x_in, cot_in = ref["x"], ref["cot"]
+    x_in, cot_in = ref.x, ref.cot
     sends = []
 
     bar = pltpu.get_barrier_semaphore()
@@ -211,7 +251,7 @@
     def owns(h):
         return frames[h] // FO == t
 
-    xb, rx, sx, fx = ref["xb"], ref["rx"], ref["sx"], ref["fx"]
+    xb, rx, sx, fx = ref.xb, ref.rx, ref.sx, ref.fx
     for p in range(N):
         c = lax.rem(i + p, N)
         for h in (0, 1):
@@ -251,7 +291,7 @@
             copy.start()
             sends.append(copy.wait_send)
 
-    cb, rc, sc = ref["cb"], ref["rc"], ref["sc"]
+    cb, rc, sc = ref.cb, ref.rc, ref.sc
     for p in range(N):
         c = lax.rem(i + p, N)
         for h in (0, 1):
@@ -278,25 +318,25 @@
 
     share = 2 * lax.rem(d, 2) + lax.rem(i, 2)
     wide = ("w_out", "w_up", "w_down")
-    full = {n: ref[n + "_full"] for n in wide + ("bias",)}
-    rw, sw, lw = ref["rw"], ref["sw"], ref["lw"]
+    full = {n: getattr(ref, n + "_full") for n in wide + ("bias",)}
+    rw, sw, lw = ref.rw, ref.sw, ref.lw
     own_copies = []
     for n, name in enumerate(wide + ("bias",)):
-        copy = pltpu.make_async_copy(ref[name], full[name].at[t], lw.at[n])
+        copy = pltpu.make_async_copy(getattr(ref, name), full[name].at[t], lw.at[n])
         copy.start()
         own_copies.append(copy)
     for p in range(1, T):
         to = {"tensor": lax.rem(t + p, T)}
-        copy = remote(ref["bias"], full["bias"].at[t], sw.at[3, 0, p], rw.at[3, 0, t], to)
+        copy = remote(ref.bias, full["bias"].at[t], sw.at[3, 0, p], rw.at[3, 0, t], to)
         copy.start()
         sends.append(copy.wait_send)
     for n, name in enumerate(wide):
-        quarter = ref[name].shape[0] // 4
+        quarter = getattr(ref, name).shape[0] // 4
         at = row_ds(share * quarter, quarter)
         for p in range(1, T):
             to = {"tensor": lax.rem(t + p, T)}
             copy = remote(
-                ref[name].at[at], full[name].at[t, at], sw.at[n, 0, p], rw.at[n, 0, t], to
+                getattr(ref, name).at[at], full[name].at[t, at], sw.at[n, 0, p], rw.at[n, 0, t], to
             )
             copy.start()
             sends.append(copy.wait_send)
@@ -306,7 +346,7 @@
     other_both = 2 * (1 - lax.rem(d, 2)) + 1 - lax.rem(i, 2)
 
     def weight_part(name, s, which):
-        quarter = ref[name].shape[0] // 4
+        quarter = getattr(ref, name).shape[0] // 4
         return full[name].at[s, row_ds(which * quarter, quarter)]
 
     def weights_second(n, name):
@@ -341,14 +381,14 @@
                 arrived(weight_part(name, s, other_both), rw.at[n, 3, s])
 
     RB = min(256, R)
-    nb, qb_, kb_, vb_ = ref["nb"], ref["q"], ref["k"], ref["v"]
-    vec = ref["vec"]
-    wqkv = ref["w_qkv"]
+    nb, qb_, kb_, vb_ = ref.nb, ref.q, ref.k, ref.v
+    vec = (ref.gain_attn, ref.shift_attn, ref.gain_mlp, ref.shift_mlp)
+    wqkv = ref.w_qkv
 
     def project(start):
         rows = row_ds(start, RB, 64)
         xhat, _ = norm_parts(xb[rows, :].astype(F32))
-        normed = (xhat * vec[0:1, :] + vec[1:2, :]).astype(BF)
+        normed = (xhat * vec[0][...] + vec[1][...]).astype(BF)
         nb[rows, :] = normed
         packed = dot(normed, wqkv[...])
         for g in range(G):
@@ -370,9 +410,9 @@
     for n, name in enumerate(wide):
         weights_second(n, name)
 
-    live = ref["live"][i]
-    probs, mo, mr = ref["probs"], ref["mo"], ref["mr"]
-    rm, sm = ref["rm"], ref["sm"]
+    live = ref.live[i]
+    probs, mo, mr = ref.probs, ref.mo, ref.mr
+    rm, sm = ref.rm, ref.sm
     piece = min(QB, R)
     NQ = L // QB
     lane = lax.broadcasted_iota(jnp.int32, (QB, GW), 1) // head_dim
@@ -417,27 +457,34 @@
             sends.append(done)
 
     pumps = [functools.partial(weights_third, n, name) for n, name in enumerate(wide)]
-    for qb in reversed(range(NQ)):
+    def mask_shift(qb):
         K = (qb + 1) * QB
-        rows = pl.ds(qb * QB, QB)
         row_frame = (qb * QB + lax.broadcasted_iota(jnp.int32, (QB, K), 0)) // PATCH
         col_frame = lax.broadcasted_iota(jnp.int32, (QB, K), 1) // PATCH
         allowed = (col_frame <= row_frame) & (col_frame < live)
-        shift = jnp.where(allowed, 0.0, -1e30)
+        return jnp.where(allowed, 0.0, -1e30)
+
+    def attend_block(qb, g, shift):
+        K = (qb + 1) * QB
+        rows = pl.ds(qb * QB, QB)
+        qv = qb_[g, rows, :]
+        kv = kb_[g, pl.ds(0, K), :]
+        vv = vb_[g, pl.ds(0, K), :]
+        outs = []
+        for a in range(HG):
+            scores = dot(only(qv, a), kv, NT) + shift
+            top = jnp.max(scores, axis=-1, keepdims=True)
+            weights = jnp.exp(scores - top)
+            total = jnp.sum(weights, axis=-1, keepdims=True)
+            prob = (weights * (1.0 / total)).astype(BF)
+            probs[g * HG + a, rows, pl.ds(0, K)] = prob
+            outs.append(dot(prob, vv))
+        mo[rows, pl.ds(g * GW, GW)] = pick(outs).astype(BF)
+
+    for qb in reversed(range(NQ)):
+        shift = mask_shift(qb)
         for g in range(G):
-            qv = qb_[g, rows, :]
-            kv = kb_[g, pl.ds(0, K), :]
-            vv = vb_[g, pl.ds(0, K), :]
-            outs = []
-            for a in range(HG):
-                scores = dot(only(qv, a), kv, NT) + shift
-                top = jnp.max(scores, axis=-1, keepdims=True)
-                weights = jnp.exp(scores - top)
-                total = jnp.sum(weights, axis=-1, keepdims=True)
-                prob = (weights * (1.0 / total)).astype(BF)
-                probs[g * HG + a, rows, pl.ds(0, K)] = prob
-                outs.append(dot(prob, vv))
-            mo[rows, pl.ds(g * GW, GW)] = pick(outs).astype(BF)
+            attend_block(qb, g, shift)
             hand_over(qb, g)
         if pumps:
             pumps.pop(0)()
@@ -457,11 +504,11 @@
         arrived(cb.at[pl.ds(k * tok, tok)], rc.at[k])
 
     wof, wuf, wdf, bf_ = full["w_out"], full["w_up"], full["w_down"], full["bias"]
-    second, act, gpre = ref["second"], ref["act"], ref["gpre"]
-    mlow, gmid, gst, gx = ref["mlow"], ref["gmid"], ref["gst"], ref["gx"]
-    ob, out_ref, ig_ref = ref["ob"], ref["out"], ref["ig"]
-    sv = ref["sv"]
-    mlp_sum, sec_sum = ref["mlp_sum"], ref["sec_sum"]
+    second, act, gpre = ref.second, ref.act, ref.gpre
+    mlow, gmid, gst, gx = ref.mlow, ref.gmid, ref.gst, ref.gx
+    ob, out_ref, ig_ref = ref.ob, ref.out, ref.ig
+    sv = ref.sv
+    mlp_sum, sec_sum = ref.mlp_sum, ref.sec_sum
     RC = min(256, R)
     FT = min(512, FFh)
     c0 = 0.7978845608028654
@@ -528,15 +575,15 @@
                 def _(c=c, h=h):
                     arrived(dst_ref.at[c, h], rs.at[c, h])
 
-    sg, rg = ref["sg"], ref["rg"]
-    for rc_index in range(R // RC):
+    sg, rg = ref.sg, ref.rg
+    def feed_forward(rc_index):
         rows = pl.ds(rc_index * RC, RC)
         attn = dot(mr[0, rows, :], wof[0])
         for s in range(1, T):
             attn = attn + dot(mr[s, rows, :], wof[s])
         middle = xb[row_ds(t * R + rc_index * RC, RC, 64), :].astype(F32) + attn
         xhat, rstd = norm_parts(middle)
-        sec = (xhat * vec[2:3, :] + vec[3:4, :]).astype(BF)
+        sec = (xhat * vec[2][...] + vec[3][...]).astype(BF)
         second[rows, :] = sec
         cot = cb[rows, :]
         for s in range(T):
@@ -567,12 +614,17 @@
         gsec = sec_sum[...]
         sv[0, 2:3, 0:D] = sv[0, 2:3, 0:D] + jnp.sum(gsec * xhat, axis=0, keepdims=True)
         sv[0, 3:4, 0:D] = sv[0, 3:4, 0:D] + jnp.sum(gsec, axis=0, keepdims=True)
-        gm = cot.astype(F32) + norm_back(gsec, vec[2:3, :], xhat, rstd)
+        gm = cot.astype(F32) + norm_back(gsec, vec[2][...], xhat, rstd)
         gmid[rows, :] = gm
         low = gm.astype(BF)
         mlow[rows, :] = low
         for s in range(T):
             gst[s, rows, :] = dot(low, wof[s], NT).astype(BF)
+
+    for rc_index in range(R // RC):
+        rows = pl.ds(rc_index * RC, RC)
+        feed_forward(rc_index)
+        for s in range(T):
             src = gst.at[s, rows]
             dst = gx.at[row_ds(t * R + rc_index * RC, RC, 64)]
 
@@ -595,25 +647,25 @@
 
             sends.append(done)
         for k in range(rc_index * RC // tok, (rc_index + 1) * RC // tok):
-            give_back(ob, out_ref, ref["so"], ref["ro"], k)
+            give_back(ob, out_ref, ref.so, ref.ro, k)
 
     reduces = {}
-    for name in cfg["plans"]:
-        levels = cfg["plans"][name]
-        bufs = [ref[f"{name}_buf{n}"] for n in range(len(levels))]
+    for name in cfg.plans:
+        levels = cfg.plans[name]
+        bufs = [getattr(ref, name + "_buf" + str(n)) for n in range(len(levels))]
         reduces[name] = Reduce(
-            levels, ref[name + "_acc"], ref[name + "_fin"], bufs, ref[name + "_ss"],
-            ref[name + "_rs"], place,
+            levels, getattr(ref, name + "_acc"), getattr(ref, name + "_fin"), bufs, getattr(ref, name + "_ss"),
+            getattr(ref, name + "_rs"), place,
         )
     cot = cb[...]
     for s in range(T):
-        ref["down_acc"][s] = dot(act[s], cot, TN).astype(BF)
+        ref.down_acc[s] = dot(act[s], cot, TN).astype(BF)
     reduces["down"].tick()
     for s in range(T):
-        ref["up_acc"][s] = dot(second[...], gpre[s], TN).astype(BF)
+        ref.up_acc[s] = dot(second[...], gpre[s], TN).astype(BF)
     reduces["up"].tick()
     for s in range(T):
-        ref["out_acc"][s] = dot(mr[s], mlow[...], TN).astype(BF)
+        ref.out_acc[s] = dot(mr[s], mlow[...], TN).astype(BF)
     reduces["out"].tick()
 
     for p in range(1, T):
@@ -621,41 +673,45 @@
         for n in range(R // RC):
             arrived(gx.at[row_ds(s * R + n * RC, RC, 64)], rg.at[s, n])
 
-    dk, dv, gpb = ref["dk"], ref["dv"], ref["gpb"]
+    dk, dv, gpb = ref.dk, ref.dv, ref.gpb
+
+    def attend_back_block(g, qb):
+        K = (qb + 1) * QB
+        rows = pl.ds(qb * QB, QB)
+        keys = pl.ds(0, K)
+        lanes = pl.ds(g * GW, GW)
+        go = gx[rows, lanes]
+        prod = go.astype(F32) * mo[rows, lanes].astype(F32)
+        qv = qb_[g, rows, :]
+        kv = kb_[g, keys, :]
+        vv = vb_[g, keys, :]
+        outs = []
+        dk_sum = dv_sum = None
+        for a in range(HG):
+            delta = jnp.sum(only(prod, a), axis=-1, keepdims=True)
+            goa = only(go, a)
+            prob = probs[g * HG + a, rows, keys]
+            gprob = dot(goa, vv, NT)
+            gs = (prob.astype(F32) * (gprob - delta)).astype(BF)
+            outs.append(dot(gs, kv))
+            dk_part = dot(gs, only(qv, a), TN)
+            dv_part = dot(prob, goa, TN)
+            dk_sum = dk_part if dk_sum is None else dk_sum + dk_part
+            dv_sum = dv_part if dv_sum is None else dv_sum + dv_part
+        gpb[rows, lanes] = (pick(outs) * scale).astype(BF)
+        if qb == NQ - 1:
+            dk[keys, :] = dk_sum
+            dv[keys, :] = dv_sum
+        else:
+            dk[keys, :] = dk[keys, :] + dk_sum
+            dv[keys, :] = dv[keys, :] + dv_sum
+
     turns = 0
     for g in range(G):
         for qb in reversed(range(NQ)):
-            K = (qb + 1) * QB
-            rows = pl.ds(qb * QB, QB)
-            keys = pl.ds(0, K)
-            lanes = pl.ds(g * GW, GW)
-            go = gx[rows, lanes]
-            prod = go.astype(F32) * mo[rows, lanes].astype(F32)
-            qv = qb_[g, rows, :]
-            kv = kb_[g, keys, :]
-            vv = vb_[g, keys, :]
-            outs = []
-            dk_sum = dv_sum = None
-            for a in range(HG):
-                delta = jnp.sum(only(prod, a), axis=-1, keepdims=True)
-                goa = only(go, a)
-                prob = probs[g * HG + a, rows, keys]
-                gprob = dot(goa, vv, NT)
-                gs = (prob.astype(F32) * (gprob - delta)).astype(BF)
-                outs.append(dot(gs, kv))
-                dk_part = dot(gs, only(qv, a), TN)
-                dv_part = dot(prob, goa, TN)
-                dk_sum = dk_part if dk_sum is None else dk_sum + dk_part
-                dv_sum = dv_part if dv_sum is None else dv_sum + dv_part
-            gpb[rows, lanes] = (pick(outs) * scale).astype(BF)
-            if qb == NQ - 1:
-                dk[keys, :] = dk_sum
-                dv[keys, :] = dv_sum
-            else:
-                dk[keys, :] = dk[keys, :] + dk_sum
-                dv[keys, :] = dv[keys, :] + dv_sum
+            attend_back_block(g, qb)
             if turns == 1:
-                pass_on(out_ref, ref["fo"], ref["ro"])
+                pass_on(out_ref, ref.fo, ref.ro)
             reduces["down"].tick()
             reduces["up"].tick()
             reduces["out"].tick()
@@ -663,39 +719,39 @@
         gpb[:, pl.ds(HW + g * GW, GW)] = dk[...].astype(BF)
         gpb[:, pl.ds(2 * HW + g * GW, GW)] = dv[...].astype(BF)
 
-    gns, gnr = ref["gns"], ref["gnr"]
+    gns, gnr = ref.gns, ref.gnr
     for p in range(1, T):
         s = lax.rem(t + p, T)
         gns[p - 1] = dot(gpb[row_ds(s * R, R, 64), :], wqkv[...], NT).astype(BF)
-        copy = remote(gns.at[p - 1], gnr.at[p - 1], ref["sn"].at[p - 1], ref["rn"].at[p - 1], {"tensor": s})
+        copy = remote(gns.at[p - 1], gnr.at[p - 1], ref.sn.at[p - 1], ref.rn.at[p - 1], {"tensor": s})
         copy.start()
         sends.append(copy.wait_send)
-    ref["qkv_acc"][0] = dot(nb[...], gpb[...], TN).astype(BF)
+    ref.qkv_acc[0] = dot(nb[...], gpb[...], TN).astype(BF)
     reduces["qkv"].tick()
     own = dot(gpb[row_ds(t * R, R, 64), :], wqkv[...], NT)
     for p in range(1, T):
-        arrived(gnr.at[p - 1], ref["rn"].at[p - 1])
+        arrived(gnr.at[p - 1], ref.rn.at[p - 1])
         own = own + gnr[p - 1].astype(F32)
     xhat, rstd = norm_parts(xb[row_ds(t * R, R, 64), :].astype(F32))
     sv[0, 0:1, 0:D] = jnp.sum(own * xhat, axis=0, keepdims=True)
     sv[0, 1:2, 0:D] = jnp.sum(own, axis=0, keepdims=True)
-    igb = ref["igb"]
-    igb[...] = (gmid[...] + norm_back(own, vec[0:1, :], xhat, rstd)).astype(BF)
+    igb = ref.igb
+    igb[...] = (gmid[...] + norm_back(own, vec[0][...], xhat, rstd)).astype(BF)
     for k in range(FO):
-        give_back(igb, ig_ref, ref["si"], ref["ri"], k)
-
-    rsv = ref["rsv"]
+        give_back(igb, ig_ref, ref.si, ref.ri, k)
+
+    rsv = ref.rsv
     everyone = [(a, b) for a, n in (("ctx", N), ("dp", DP), ("tensor", T)) for b in bits_of(n)]
     for n, (axis, bit) in enumerate(everyone):
         copy = remote(
-            sv.at[n], rsv.at[n], ref["sv_ss"].at[n], ref["sv_rs"].at[n],
+            sv.at[n], rsv.at[n], ref.sv_ss.at[n], ref.sv_rs.at[n],
             {axis: flip(place[axis], bit)},
         )
         copy.start()
         reduces["qkv"].tick()
         copy.wait()
         sv[n + 1] = sv[n] + rsv[n]
-    pass_on(ig_ref, ref["fi"], ref["ri"])
+    pass_on(ig_ref, ref.fi, ref.ri)
     last = sv[len(everyone)]
     part = D // T
     gains = last[0:4, 0:part]
@@ -703,15 +759,627 @@
     for s in range(1, T):
         gains = jnp.where(t == s, last[0:4, s * part : (s + 1) * part], gains)
         bias = jnp.where(t == s, last[4 + s : 5 + s, 0:FFh], bias)
-    ref["gains"][...] = gains
-    ref["bias_out"][...] = bias
+    for n, got in enumerate((ref.grad_ga, ref.grad_sa, ref.grad_gm, ref.grad_sm)):
+        got[...] = gains[n : n + 1, :]
+    ref.bias_out[...] = bias
 
     for name in ("down", "up", "out", "qkv"):
         reduces[name].drain()
-    take_rest(out_ref, ref["ro"])
-    take_rest(ig_ref, ref["ri"])
+    take_rest(out_ref, ref.ro)
+    take_rest(ig_ref, ref.ri)
     for done in sends:
         done()
+
+
+def chip_kernel(cfg, names, *refs):
+    ref = SimpleNamespace(**dict(zip(names, refs)))
+    N, T, DP = cfg.N, cfg.T, cfg.DP
+    L, R, FO, tok = cfg.L, cfg.R, cfg.FO, cfg.tok
+    D, HW, GW, G, FFh, QB = cfg.D, cfg.HW, cfg.GW, cfg.G, cfg.FFh, cfg.QB
+    head_dim = cfg.head_dim
+    Z = N // 2
+    HG = GW // head_dim
+    scale = head_dim ** (-0.5)
+    d = lax.axis_index("dp")
+    i = lax.axis_index("ctx")
+    t = lax.axis_index("tensor")
+    z, kap = i // 2, lax.rem(i, 2)
+    clip = 2 * z + t
+    mate, mirror, beside = {"ctx": flip(i, 1)}, {"tensor": 1 - t}, {"dp": flip(d, 1)}
+    place = {"dp": d, "ctx": i, "tensor": t}
+    x_in, cot_in = ref.x, ref.cot
+    sends = []
+
+    def go(src, dst, send_sem, recv_sem, where):
+        copy = remote(src, dst, send_sem, recv_sem, where)
+        copy.start()
+        sends.append(copy.wait_send)
+
+    def go_if(cond, *args):
+        @pl.when(cond)
+        def _():
+            remote(*args).start()
+
+        def done():
+            @pl.when(cond)
+            def _():
+                remote(*args).wait_send()
+
+        sends.append(done)
+
+    bar = pltpu.get_barrier_semaphore()
+    peers = [{"ctx": lax.rem(i + p, N)} for p in range(1, N)]
+    peers += [mirror] + [{"dp": flip(d, b)} for b in bits_of(DP)]
+    for peer in peers:
+        pl.semaphore_signal(bar, inc=1, device_id=peer, device_id_type=MESH)
+
+    wqkv, rq = ref.wq, ref.rq
+    blocks = []
+    for n in range(HW // head_dim):
+        for b in range(3):
+            src = ref.w_qkv.at[n, pl.ds(b * head_dim, head_dim)]
+            dst = wqkv.at[pl.ds(b * HW + n * head_dim, head_dim)]
+            blocks.append((src, dst, ref.bq.at[3 * n + b]))
+
+    @pl.when(kap == t)
+    def _():
+        for block in blocks:
+            pltpu.make_async_copy(*block).start()
+        for block in blocks:
+            pltpu.make_async_copy(*block).wait()
+
+    pl.semaphore_wait(bar, len(peers))
+
+    frames = (i, 2 * N - 1 - i)
+
+    def deal(src_ref, dst_ref, spot, ss, rs):
+        for p in range(Z):
+            zz = lax.rem(z + p, Z)
+            for h in (0, 1):
+                src = src_ref.at[2 * zz + t, h]
+                dst = dst_ref.at[row_ds(spot(h) * tok, tok)]
+                to = {"ctx": 2 * zz + h}
+                sem = rs.at[spot(h)]
+                if p == 0:
+
+                    @pl.when(kap == h)
+                    def _(src=src, dst=dst, sem=sem):
+                        pltpu.make_async_copy(src, dst, sem).start()
+
+                    go_if(kap != h, src, dst, ss.at[p, h], sem, to)
+                else:
+                    go(src, dst, ss.at[p, h], sem, to)
+
+    xb, rx = ref.xb, ref.rx
+    deal(x_in, xb, lambda h: frames[h], ref.sx, rx)
+    cb, rc = ref.cb, ref.rc
+    deal(cot_in, cb, lambda h: frames[h] - h * FO, ref.sc, rc)
+
+    half = 3 * HW // 2
+    first_half = row_ds(lax.rem(d, 2) * half, half)
+    other_half = row_ds((1 - lax.rem(d, 2)) * half, half)
+    go_if(
+        kap == t, wqkv.at[first_half], wqkv.at[first_half], ref.sq.at[0], rq.at[1],
+        mirror,
+    )
+
+    share = 2 * lax.rem(d, 2) + kap
+    other_dp = 2 * (1 - lax.rem(d, 2)) + kap
+    other_core = 2 * lax.rem(d, 2) + 1 - kap
+    other_both = 2 * (1 - lax.rem(d, 2)) + 1 - kap
+    wide = ("w_out", "w_up", "w_down")
+    full = {n: getattr(ref, n + "_full") for n in wide + ("bias",)}
+    rw, sw, lw = ref.rw, ref.sw, ref.lw
+    own_copies = {}
+    for n, name in enumerate(wide + ("bias",)):
+        own_copies[name] = pltpu.make_async_copy(getattr(ref, name), full[name].at[t], lw.at[n])
+        own_copies[name].start()
+
+    def weight_part(name, s, which):
+        quarter = getattr(ref, name).shape[0] // 4
+        return full[name].at[s, row_ds(which * quarter, quarter)]
+
+    for n, name in enumerate(wide):
+        quarter = getattr(ref, name).shape[0] // 4
+        src = getattr(ref, name).at[row_ds(share * quarter, quarter)]
+        go(src, weight_part(name, t, share), sw.at[n, 0], rw.at[n, 0], mirror)
+    go(ref.bias, full["bias"].at[t], sw.at[3, 0], rw.at[3, 0], mirror)
+
+    def weights_second(name):
+        n = wide.index(name)
+        part = weight_part(name, 1 - t, share)
+        arrived(part, rw.at[n, 0])
+        go(part, part, sw.at[n, 1], rw.at[n, 1], beside)
+        go(part, part, sw.at[n, 2], rw.at[n, 2], mate)
+
+    def weights_third(name):
+        n = wide.index(name)
+        part = weight_part(name, 1 - t, other_dp)
+        arrived(part, rw.at[n, 1])
+        go(part, part, sw.at[n, 3], rw.at[n, 3], mate)
+
+    def weights_ready(name):
+        n = wide.index(name)
+        arrived(weight_part(name, 1 - t, other_core), rw.at[n, 2])
+        arrived(weight_part(name, 1 - t, other_both), rw.at[n, 3])
+
+    RB = min(256, R)
+    nb, qb_, kb_, vb_ = ref.nb, ref.q, ref.k, ref.v
+    vec = (ref.gain_attn, ref.shift_attn, ref.gain_mlp, ref.shift_mlp)
+
+    def project(start):
+        rows = row_ds(start, RB, 64)
+        xhat, _ = norm_parts(xb[rows, :].astype(F32))
+        normed = (xhat * vec[0][...] + vec[1][...]).astype(BF)
+        nb[rows, :] = normed
+        packed = dot(normed, wqkv[...], NT)
+        for g in range(G):
+            lo = g * GW
+            qb_[g, rows, :] = (packed[:, lo : lo + GW].astype(BF).astype(F32) * scale).astype(BF)
+            kb_[g, rows, :] = packed[:, HW + lo : HW + lo + GW].astype(BF)
+            vb_[g, rows, :] = packed[:, 2 * HW + lo : 2 * HW + lo + GW].astype(BF)
+
+    @pl.when(kap != t)
+    def _():
+        arrived(wqkv.at[first_half], rq.at[1])
+
+    go_if(
+        kap != t, wqkv.at[first_half], wqkv.at[first_half], ref.sq.at[1], rq.at[2], beside
+    )
+    weights_second("w_out")
+    for p in range(Z):
+        for core in (0, 1):
+            j = 2 * lax.rem(z + p, Z) + core
+            f = j * (1 - kap) + (2 * N - 1 - j) * kap
+            part = xb.at[row_ds(f * tok, tok)]
+            arrived(part, rx.at[f])
+            go(part, part, ref.fx.at[p, core], rx.at[f], mate)
+
+    @pl.when(kap != t)
+    def _():
+        arrived(wqkv.at[other_half], rq.at[2])
+
+    for k in range(R // RB):
+        project(kap * R + k * RB)
+    for k in range(FO):
+        f = (1 - kap) * FO + k
+        arrived(xb.at[row_ds(f * tok, tok)], rx.at[f])
+    for k in range(R // RB):
+        project((1 - kap) * R + k * RB)
+
+    live = ref.live[clip]
+    probs, mo, mr = ref.probs, ref.mo, ref.mr
+    rm, sm = ref.rm, ref.sm
+    NQ = L // QB
+    lane = lax.broadcasted_iota(jnp.int32, (QB, GW), 1) // head_dim
+
+    def pick(parts):
+        out = parts[0]
+        for a in range(1, HG):
+            out = jnp.where(lane == a, parts[a], out)
+        return out
+
+    def only(values, a):
+        if HG == 1:
+            return values
+        return jnp.where(lane == a, values, jnp.zeros_like(values))
+
+    def hand_over(qb, g):
+        row = qb * QB
+        s = row // R
+        off = row - s * R
+        lanes = pl.ds(g * GW, GW)
+        src = mo.at[pl.ds(row, QB), lanes]
+        dst = mr.at[kap, pl.ds(off, QB), lanes]
+
+        @pl.when(kap == s)
+        def _():
+            mr[kap, pl.ds(off, QB), lanes] = mo[pl.ds(row, QB), lanes]
+
+        go_if(kap != s, src, dst, sm.at[qb, g], rm.at[off // QB, g], mate)
+
+    def mask_shift(qb):
+        K = (qb + 1) * QB
+        row_frame = (qb * QB + lax.broadcasted_iota(jnp.int32, (QB, K), 0)) // PATCH
+        col_frame = lax.broadcasted_iota(jnp.int32, (QB, K), 1) // PATCH
+        allowed = (col_frame <= row_frame) & (col_frame < live)
+        return jnp.where(allowed, 0.0, -1e30)
+
+    def attend_block(qb, g, shift):
+        K = (qb + 1) * QB
+        rows = pl.ds(qb * QB, QB)
+        qv = qb_[g, rows, :]
+        kv = kb_[g, pl.ds(0, K), :]
+        vv = vb_[g, pl.ds(0, K), :]
+        outs = []
+        for a in range(HG):
+            scores = dot(only(qv, a), kv, NT) + shift
+            top = jnp.max(scores, axis=-1, keepdims=True)
+            weights = jnp.exp(scores - top)
+            total = jnp.sum(weights, axis=-1, keepdims=True)
+            prob = (weights * (1.0 / total)).astype(BF)
+            probs[g * HG + a, rows, pl.ds(0, K)] = prob
+            outs.append(dot(prob, vv))
+        mo[rows, pl.ds(g * GW, GW)] = pick(outs).astype(BF)
+
+    pumps = {
+        (0, 0): functools.partial(weights_second, "w_up"),
+        (1, 1): functools.partial(weights_second, "w_down"),
+        (2, 0): functools.partial(weights_third, "w_out"),
+    }
+    for qb in range(NQ):
+        shift = mask_shift(qb)
+        for g in range(G):
+            attend_block(qb, g, shift)
+            hand_over(qb, g)
+            if (qb, g) in pumps:
+                pumps[qb, g]()
+
+    wof, wuf, wdf, bf_ = full["w_out"], full["w_up"], full["w_down"], full["bias"]
+    second, act, gpre = ref.second, ref.act, ref.gpre
+    mlow, gmid, gst, gx = ref.mlow, ref.gmid, ref.gst, ref.gx
+    ob, out_ref, ig_ref = ref.ob, ref.out, ref.ig
+    mid, bsum, sv = ref.mid, ref.bsum, ref.sv
+    mlp_sum, sec_sum = ref.mlp_sum, ref.sec_sum
+    RC = min(256, R)
+    FT = min(512, FFh)
+    c0 = 0.7978845608028654
+
+    def middle_rows(c):
+        rows = pl.ds(c * RC, RC)
+        attn = dot(mr[0, rows, :], wof[0])
+        for s in range(1, T):
+            attn = attn + dot(mr[s, rows, :], wof[s])
+        middle = xb[row_ds(kap * R + c * RC, RC, 64), :].astype(F32) + attn
+        mid[rows, :] = middle
+        xhat, _ = norm_parts(middle)
+        second[rows, :] = (xhat * vec[2][...] + vec[3][...]).astype(BF)
+
+    def feed_forward(s, c, first):
+        rows = pl.ds(c * RC, RC)
+        sec = second[rows, :]
+        cot = cb[rows, :]
+        for j in range(FFh // FT):
+            cols = pl.ds(j * FT, FT)
+            pre = dot(sec, wuf[s, :, cols]) + bf_[s, 0:1, cols]
+            gact = dot(cot, wdf[s, cols, :], NT)
+            sq = pre * pre
+            th = jnp.tanh(c0 * pre * (1.0 + 0.044715 * sq))
+            half = 0.5 * (1.0 + th)
+            a = (pre * half).astype(BF)
+            slope = half + 0.5 * pre * (1.0 - th * th) * (c0 * (1.0 + 0.134145 * sq))
+            gp = (gact * slope).astype(BF)
+            act[s, rows, cols] = a
+            gpre[s, rows, cols] = gp
+            sums = jnp.sum(gp.astype(F32), axis=0, keepdims=True)
+            bsum[s, 0:1, cols] = sums if c == 0 else bsum[s, 0:1, cols] + sums
+            up = dot(a, wdf[s, cols, :])
+            back = dot(gp, wuf[s, :, cols], NT)
+            if first and j == 0:
+                mlp_sum[rows, :] = up
+                sec_sum[rows, :] = back
+            else:
+                mlp_sum[rows, :] = mlp_sum[rows, :] + up
+                sec_sum[rows, :] = sec_sum[rows, :] + back
+
+    def finish_rows(c):
+        rows = pl.ds(c * RC, RC)
+        middle = mid[rows, :]
+        xhat, rstd = norm_parts(middle)
+        ob[rows, :] = (middle + mlp_sum[rows, :]).astype(BF)
+        gsec = sec_sum[rows, :]
+        gain_sum = jnp.sum(gsec * xhat, axis=0, keepdims=True)
+        shift_sum = jnp.sum(gsec, axis=0, keepdims=True)
+        if c > 0:
+            gain_sum = gain_sum + sv[0, 2:3, 0:D]
+            shift_sum = shift_sum + sv[0, 3:4, 0:D]
+        sv[0, 2:3, 0:D] = gain_sum
+        sv[0, 3:4, 0:D] = shift_sum
+        gm = cb[rows, :].astype(F32) + norm_back(gsec, vec[2][...], xhat, rstd)
+        gmid[rows, :] = gm
+        low = gm.astype(BF)
+        mlow[rows, :] = low
+        for s in range(T):
+            gst[s, rows, :] = dot(low, wof[s], NT).astype(BF)
+
+    def give_back(buf, dst_ref, ss, rs, k):
+        f = kap * FO + k
+        j = f * (1 - kap) + (2 * N - 1 - f) * kap
+        src = buf.at[pl.ds(k * tok, tok)]
+        dst, sem = dst_ref.at[clip, kap], rs.at[clip, kap]
+
+        @pl.when(j == i)
+        def _():
+            pltpu.make_async_copy(src, dst, sem).start()
+
+        go_if(j != i, src, dst, ss.at[k], sem, {"ctx": j})
+
+    def pass_on(dst_ref, fs, rs, p):
+        for h in (0, 1):
+            cc = 2 * lax.rem(z + p, Z) + t
+            part = dst_ref.at[cc, h]
+            arrived(part, rs.at[cc, h])
+            go(part, part, fs.at[p, h], rs.at[cc, h], mirror)
+
+    def take_rest(dst_ref, rs):
+        for p in range(Z):
+            for h in (0, 1):
+                cc = 2 * p + 1 - t
+                arrived(dst_ref.at[cc, h], rs.at[cc, h])
+
+    down_fin, up_fin = ref.down_fin, ref.up_fin
+    fins = {
+        "down0": down_fin.at[pl.ds(0, FFh // 2)],
+        "down1": down_fin.at[pl.ds(FFh // 2, FFh // 2)],
+        "up0": up_fin.at[pl.ds(0, D // 2)],
+        "up1": up_fin.at[pl.ds(D // 2, D // 2)],
+        "out": ref.out_fin,
+        "qkv0": ref.qkv_fin.at[0],
+        "qkv1": ref.qkv_fin.at[1],
+    }
+    reduces = {}
+    for name, levels in cfg.plans.items():
+        bufs = [getattr(ref, name + "_buf" + str(n), None) for n in range(len(levels))]
+        reduces[name] = Reduce(
+            levels, getattr(ref, name + "_acc"), fins[name], bufs, getattr(ref, name + "_ss"),
+            getattr(ref, name + "_rs"), place,
+        )
+
+    def grad_wide(name, s):
+        k = int(name[-1])
+        if name[0] == "d":
+            cols = pl.ds(k * (FFh // 2), FFh // 2)
+            getattr(ref, name + "_acc")[s] = dot(act[s, :, cols], cb[...], TN).astype(BF)
+        else:
+            cols = pl.ds(k * (D // 2), D // 2)
+            getattr(ref, name + "_acc")[s] = dot(second[:, cols], gpre[s], TN).astype(BF)
+
+    rsv = ref.rsv
+    everyone = [("ctx", b) for b in bits_of(N)] + [("dp", b) for b in bits_of(DP)]
+    everyone += [("tensor", b) for b in bits_of(T)]
+    vec_copy = []
+
+    def vec_step():
+        n = len(vec_copy)
+        if n > 0:
+            vec_copy[-1].wait()
+            sv[n] = sv[n - 1] + rsv[n - 1]
+        if n < len(everyone):
+            axis, bit = everyone[n]
+            copy = remote(
+                sv.at[n], rsv.at[n], ref.sv_ss.at[n], ref.sv_rs.at[n],
+                {axis: flip(place[axis], bit)},
+            )
+            copy.start()
+            vec_copy.append(copy)
+        else:
+            vec_copy.append(None)
+
+    out_done, ig_done = [], []
+    script = list(cfg.script)
+
+    def run_script():
+        while script:
+            item = script.pop(0)
+            if item == MARK:
+                return
+            if item == VECTORS:
+                vec_step()
+            elif item == OUTPUT:
+                pass_on(out_ref, ref.fo, ref.ro, len(out_done))
+                out_done.append(item)
+            elif item == INPUT_GRAD:
+                pass_on(ig_ref, ref.fi, ref.ri, len(ig_done))
+                ig_done.append(item)
+            else:
+                reduces[CHUNKS[item]].tick()
+
+    for name in wide + ("bias",):
+        own_copies[name].wait()
+    arrived(full["bias"].at[1 - t], rw.at[3, 0])
+    weights_ready("w_out")
+    for k in range(FO):
+        arrived(cb.at[pl.ds(k * tok, tok)], rc.at[k])
+    for c in range(R // RC):
+        for g in range(G):
+            rows, lanes = pl.ds(c * RC, RC), pl.ds(g * GW, GW)
+            arrived(mr.at[1 - kap, rows, lanes], rm.at[c, g])
+        middle_rows(c)
+        feed_forward(t, c, True)
+        if c == 0:
+            weights_third("w_up")
+    for name in cfg.order:
+        grad_wide(name, t)
+    weights_third("w_down")
+    weights_ready("w_up")
+    weights_ready("w_down")
+    for c in range(R // RC):
+        feed_forward(1 - t, c, False)
+    sv[0, 4:5, 0:FFh] = bsum[0, 0:1, :]
+    sv[0, 5:6, 0:FFh] = bsum[1, 0:1, :]
+    sg, rg = ref.sg, ref.rg
+    for c in range(R // RC):
+        finish_rows(c)
+        rows = pl.ds(c * RC, RC)
+        home = row_ds(kap * R + c * RC, RC, 64)
+        gx[home, :] = gst[kap, rows, :]
+        go(gst.at[1 - kap, rows], gx.at[home], sg.at[c], rg.at[c], mate)
+    for k in range(FO):
+        give_back(ob, out_ref, ref.so, ref.ro, k)
+
+    for name in cfg.order:
+        grad_wide(name, 1 - t)
+        reduces[name].tick()
+    for s in range(T):
+        ref.out_acc[s] = dot(mr[s], mlow[...], TN).astype(BF)
+    reduces["out"].tick()
+    for c in range(R // RC):
+        arrived(gx.at[row_ds((1 - kap) * R + c * RC, RC, 64)], rg.at[c])
+
+    dk, dv, gpb = ref.dk, ref.dv, ref.gpb
+
+    def attend_back_block(g, qb):
+        K = (qb + 1) * QB
+        rows = pl.ds(qb * QB, QB)
+        keys = pl.ds(0, K)
+        lanes = pl.ds(g * GW, GW)
+        grad = gx[rows, lanes]
+        prod = grad.astype(F32) * mo[rows, lanes].astype(F32)
+        qv = qb_[g, rows, :]
+        kv = kb_[g, keys, :]
+        vv = vb_[g, keys, :]
+        outs = []
+        dk_sum = dv_sum = None
+        for a in range(HG):
+            delta = jnp.sum(only(prod, a), axis=-1, keepdims=True)
+            goa = only(grad, a)
+            prob = probs[g * HG + a, rows, keys]
+            gprob = dot(goa, vv, NT)
+            gs = (prob.astype(F32) * (gprob - delta)).astype(BF)
+            outs.append(dot(gs, kv))
+            dk_part = dot(gs, only(qv, a), TN)
+            dv_part = dot(prob, goa, TN)
+            dk_sum = dk_part if dk_sum is None else dk_sum + dk_part
+            dv_sum = dv_part if dv_sum is None else dv_sum + dv_part
+        gpb[rows, lanes] = (pick(outs) * scale).astype(BF)
+        if qb == NQ - 1:
+            dk[keys, :] = dk_sum
+            dv[keys, :] = dv_sum
+        else:
+            dk[keys, :] = dk[keys, :] + dk_sum
+            dv[keys, :] = dv[keys, :] + dv_sum
+
+    run_script()
+    for g in range(G):
+        for qb in reversed(range(NQ)):
+            attend_back_block(g, qb)
+            if qb == 0:
+                gpb[:, pl.ds(HW + g * GW, GW)] = dk[...].astype(BF)
+                gpb[:, pl.ds(2 * HW + g * GW, GW)] = dv[...].astype(BF)
+                for b in range(3):
+                    getattr(ref, "qkv" + str(g) + "_acc")[kap, pl.ds(b * GW, GW), :] = dot(
+                        gpb[:, pl.ds(b * HW + g * GW, GW)], nb[...], TN
+                    ).astype(BF)
+                reduces["qkv" + str(g)].tick()
+            run_script()
+
+    gns, gnr = ref.gns, ref.gnr
+    gns[...] = dot(gpb[row_ds((1 - kap) * R, R, 64), :], wqkv[...]).astype(BF)
+    go(gns, gnr, ref.sn.at[0], ref.rn.at[0], mate)
+    run_script()
+    own = dot(gpb[row_ds(kap * R, R, 64), :], wqkv[...])
+    arrived(gnr, ref.rn.at[0])
+    own = own + gnr[...].astype(F32)
+    xhat, rstd = norm_parts(xb[row_ds(kap * R, R, 64), :].astype(F32))
+    sv[0, 0:1, 0:D] = jnp.sum(own * xhat, axis=0, keepdims=True)
+    sv[0, 1:2, 0:D] = jnp.sum(own, axis=0, keepdims=True)
+    igb = ref.igb
+    igb[...] = (gmid[...] + norm_back(own, vec[0][...], xhat, rstd)).astype(BF)
+    for k in range(FO):
+        give_back(igb, ig_ref, ref.si, ref.ri, k)
+    vec_step()
+    run_script()
+    last = sv[len(everyone)]
+    part = D // T
+    gains = last[0:4, 0:part]
+    bias = last[4:5, 0:FFh]
+    for s in range(1, T):
+        gains = jnp.where(t == s, last[0:4, s * part : (s + 1) * part], gains)
+        bias = jnp.where(t == s, last[4 + s : 5 + s, 0:FFh], bias)
+    for n, got in enumerate((ref.grad_ga, ref.grad_sa, ref.grad_gm, ref.grad_sm)):
+        got[...] = gains[n : n + 1, :]
+    ref.bias_out[...] = bias
+
+    take_rest(out_ref, ref.ro)
+    take_rest(ig_ref, ref.ri)
+    for done in sends:
+        done()
+
+
+def finish_kernel(sizes, *refs):
+    D, HW, FFh, GW, G, head_dim = sizes
+    ins, outs, scratch = refs[:11], refs[11:22], refs[22:]
+    out, ig, ga, sa, qkv, wo, gm, sm, up, bias, down = ins
+    b_out, b_ig, b_qkv, b_wo, b_up, b_down, f_qkv, f_wo, f_up, f_down, sem = scratch
+    moves = []
+
+    def move(n, src, dst):
+        copy = pltpu.make_async_copy(src, dst, sem.at[n])
+        copy.start()
+        moves.append(copy)
+        return copy
+
+    half = down.shape[0] // 2
+    reads = [
+        move(0, down.at[pl.ds(0, half)], b_down.at[pl.ds(0, half)]),
+        move(1, down.at[pl.ds(half, half)], b_down.at[pl.ds(half, half)]),
+        move(2, up.at[pl.ds(0, D // 2)], b_up.at[pl.ds(0, D // 2)]),
+        move(3, up.at[pl.ds(D // 2, D // 2)], b_up.at[pl.ds(D // 2, D // 2)]),
+        move(4, wo, b_wo),
+        move(5, qkv, b_qkv),
+        move(11, out, b_out),
+        move(12, ig, b_ig),
+    ]
+    parts = (
+        (b_down, f_down, outs[10], 0, half),
+        (b_down, f_down, outs[10], half, half),
+        (b_up, f_up, outs[8], 0, D // 2),
+        (b_up, f_up, outs[8], D // 2, D // 2),
+        (b_wo, f_wo, outs[5], 0, HW),
+    )
+    for n, (src, mid, dst, off, rows) in enumerate(parts):
+        reads[n].wait()
+        at = pl.ds(off, rows)
+        mid[at, :] = src[at, :].astype(F32)
+        move(6 + n, mid.at[at], dst.at[at])
+    for n, (src, dst) in enumerate(((ga, 2), (sa, 3), (gm, 6), (sm, 7), (bias, 9))):
+        outs[dst][...] = src[...]
+    reads[6].wait()
+    move(14, b_out, outs[0])
+    reads[7].wait()
+    move(15, b_ig, outs[1])
+    reads[5].wait()
+    for g in range(G):
+        for a in range(GW // head_dim):
+            for b in range(3):
+                f_qkv[g * (GW // head_dim) + a, pl.ds(b * head_dim, head_dim), :] = b_qkv[
+                    g, pl.ds(b * GW + a * head_dim, head_dim), :
+                ].astype(F32)
+    move(13, f_qkv, outs[4])
+    for copy in moves[len(reads) :]:
+        copy.wait()
+
+
+def finish(got, layout, qkv_shape, sizes, T):
+    D, HW, FFh, GW, G, head_dim = sizes
+    vm = pl.BlockSpec(memory_space=pltpu.VMEM)
+    hbm = pl.BlockSpec(memory_space=pl.ANY)
+    S, V = jax.ShapeDtypeStruct, pltpu.VMEM
+    small = S((1, D // T), F32)
+    by_head = (qkv_shape[1], qkv_shape[2], qkv_shape[0])
+    results = pl.pallas_call(
+        functools.partial(finish_kernel, sizes),
+        out_shape=[
+            S(got.out.shape, BF), S(got.ig.shape, BF), small, small, S(by_head, F32),
+            S((HW, D), F32), small, small, S((D, FFh), F32), S((1, FFh), F32), S((FFh, D), F32),
+        ],
+        in_specs=[hbm, hbm, vm, vm, hbm, hbm, vm, vm, hbm, vm, hbm],
+        out_specs=[hbm, hbm, vm, vm, hbm, hbm, vm, vm, hbm, vm, hbm],
+        scratch_shapes=[
+            V(got.out.shape, BF), V(got.ig.shape, BF), V((G, 3 * GW, D), BF), V((HW, D), BF), V((D, FFh), BF), V((FFh, D), BF),
+            V(by_head, F32), V((HW, D), F32), V((D, FFh), F32), V((FFh, D), F32),
+            pltpu.SemaphoreType.DMA((16,)),
+        ],
+        compiler_params=pltpu.CompilerParams(vmem_limit_bytes=60 * 2**20),
+    )(
+        got.out, got.ig, got.grad_ga, got.grad_sa, got.qkv_fin, got.out_fin, got.grad_gm,
+        got.grad_sm, got.up_fin, got.bias_out, got.down_fin,
+    )
+    out, ig, ga, sa, qkv, wo, gm, sm, up, bias, down = results
+    return (
+        out.reshape(layout), ig.reshape(layout), ga[0], sa[0], qkv.transpose(2, 0, 1), wo, gm[0], sm[0], up, bias[0],
+        down,
+    )
 
 
 def body(
@@ -736,121 +1404,160 @@
     GW = min(128, HW)
     FFh = w_up.shape[1]
     L = 2 * N * tok
-    R = L // T
-    cfg = dict(
-        N=N, T=T, DP=DP, L=L, R=R, FO=2 * N // T, tok=tok, D=D, HW=HW, GW=GW, G=HW // GW,
+    by_chip = T == 2 and HW == 256 and N >= 8 and N % 2 == 0 and C == N and DP == 2 and L % 512 == 0
+    S_ = 2 if by_chip else T
+    R = L // S_
+    cfg = SimpleNamespace(
+        N=N, T=T, DP=DP, L=L, R=R, FO=2 * N // S_, tok=tok, D=D, HW=HW, GW=GW, G=HW // GW,
         FFh=FFh, QB=256, head_dim=head_dim,
     )
-    G = cfg["G"]
+    G = cfg.G
     core, rest = [("ctx", 1)], [("ctx", b) for b in bits_of(N)[1:]]
     over_dp = [("dp", b) for b in bits_of(DP)]
     over_t = [("tensor", b) for b in reversed(bits_of(T))]
-    cfg["plans"] = plans = {
-        "down": plan_levels(T, FFh, core + over_dp + over_t + rest),
-        "up": plan_levels(T, D, core + over_t + over_dp + rest),
-        "out": plan_levels(T, HW, core + over_t + over_dp + rest),
-        "qkv": plan_levels(1, D, core + over_dp + rest),
-    }
-    widths = {"down": D, "up": FFh, "out": D, "qkv": 3 * HW}
-    leads = {"down": (T, FFh), "up": (T, D), "out": (T, HW), "qkv": (1, D)}
+    if by_chip:
+        steps = {
+            "x": over_dp, "y": over_t, "z": rest[:1], "Z": rest[1:-1] + [rest[-1] + ("f",)],
+            "R": rest[1:], "X": [over_dp[-1] + ("f",)],
+        }
+        cfg.plans = plans = {}
+        cfg.script, cfg.order = SCRIPT, ORDER
+        leads, widths = {}, {}
+        for name, order in ORDERS.items():
+            begin = [("ctx", 1, "p")] if name[0] == "q" else core
+            if name[0] == "d":
+                leads[name], widths[name] = (T, FFh // 2), D
+            elif name[0] == "u":
+                leads[name], widths[name] = (T, D // 2), FFh
+            elif name[0] == "o":
+                leads[name], widths[name] = (T, HW), D
+            else:
+                leads[name], widths[name] = (T, 3 * GW), D
+            plans[name] = plan_levels(*leads[name], begin + sum((steps[c] for c in order), []))
+    else:
+        cfg.plans = plans = {
+            "down": plan_levels(T, FFh, core + over_dp + over_t + rest),
+            "up": plan_levels(T, D, core + over_t + over_dp + rest),
+            "out": plan_levels(T, HW, core + over_t + over_dp + rest),
+            "qkv": plan_levels(1, D, core + over_dp + rest),
+        }
+        leads = {"down": (T, FFh), "up": (T, D), "out": (T, HW), "qkv": (1, D)}
+        widths = {"down": D, "up": FFh, "out": D, "qkv": 3 * HW}
 
     x = inputs.reshape(C, 2, tok, D)
     cot = cotangent.reshape(C, 2, tok, D)
-    wq = w_qkv.reshape(D, heads, 3, head_dim).transpose(0, 2, 1, 3).reshape(D, 3 * HW)
-    vec = jnp.stack([gain_attn, shift_attn, gain_mlp, shift_mlp] * 2)
-    bias = jnp.broadcast_to(up_bias[None], (8, FFh))
+    wq = w_qkv.transpose(1, 2, 0)
+    if not by_chip:
+        wq = w_qkv.reshape(D, heads, 3, head_dim).transpose(0, 2, 1, 3).reshape(D, 3 * HW)
 
     vm = pl.BlockSpec(memory_space=pltpu.VMEM)
     hbm = pl.BlockSpec(memory_space=pl.ANY)
-    ins = [
-        ("x", x, hbm),
-        ("cot", cot, hbm),
-        ("live", live_frames, pl.BlockSpec(memory_space=pltpu.SMEM)),
-        ("vec", vec, vm),
-        ("w_qkv", wq, vm),
-        ("w_out", w_out, hbm),
-        ("w_up", w_up, hbm),
-        ("w_down", w_down, hbm),
-        ("bias", bias, vm),
-    ]
+    ins = dict(
+        x=(x, hbm),
+        cot=(cot, hbm),
+        live=(live_frames, pl.BlockSpec(memory_space=pltpu.SMEM)),
+        gain_attn=(gain_attn.reshape(1, D), vm),
+        shift_attn=(shift_attn.reshape(1, D), vm),
+        gain_mlp=(gain_mlp.reshape(1, D), vm),
+        shift_mlp=(shift_mlp.reshape(1, D), vm),
+        w_qkv=(wq, hbm if by_chip else vm),
+        w_out=(w_out, hbm),
+        w_up=(w_up, hbm),
+        w_down=(w_down, hbm),
+        bias=(up_bias.reshape(1, FFh), vm),
+    )
     S = jax.ShapeDtypeStruct
-    outs = [
-        ("out", S((C, 2, tok, D), BF)),
-        ("ig", S((C, 2, tok, D), BF)),
-        ("down_fin", S((FFh, D), BF)),
-        ("up_fin", S((D, FFh), BF)),
-        ("out_fin", S((HW, D), BF)),
-        ("qkv_fin", S((D, 3 * HW), BF)),
-        ("gains", S((4, D // T), F32)),
-        ("bias_out", S((1, FFh), F32)),
-    ]
+    outs = dict(
+        out=S((C, 2, tok, D), BF),
+        ig=S((C, 2, tok, D), BF),
+        down_fin=S((FFh, D), BF),
+        up_fin=S((D, FFh), BF),
+        out_fin=S((HW, D), BF),
+        qkv_fin=S((G, 3 * GW, D) if by_chip else (D, 3 * HW), BF),
+        grad_ga=S((1, D // T), F32),
+        grad_sa=S((1, D // T), F32),
+        grad_gm=S((1, D // T), F32),
+        grad_sm=S((1, D // T), F32),
+        bias_out=S((1, FFh), F32),
+    )
     W = max(D, FFh)
     SR = -(-(4 + T) // 8) * 8
     n_all = len(bits_of(N)) + len(bits_of(DP)) + len(bits_of(T))
     RC = min(256, R)
-    piece = min(cfg["QB"], R)
-    FO = cfg["FO"]
+    piece = min(cfg.QB, R)
+    FO = cfg.FO
     dma = pltpu.SemaphoreType.DMA
     V = pltpu.VMEM
     scratch = dict(
-        xb=V((L, D), BF), rx=dma((2 * N,)), sx=dma((N, 2)), fx=dma((T, FO)),
-        cb=V((R, D), BF), rc=dma((FO,)), sc=dma((N, 2)),
+        xb=V((L, D), BF), rx=dma((2 * N,)),
+        cb=V((R, D), BF), rc=dma((FO,)),
         w_out_full=V((T, HW, D), BF), w_up_full=V((T, D, FFh), BF),
-        w_down_full=V((T, FFh, D), BF), bias_full=V((T, 8, FFh), F32),
-        rw=dma((4, 4, T)), sw=dma((4, 4, T)), lw=dma((4,)),
+        w_down_full=V((T, FFh, D), BF), bias_full=V((T, 1, FFh), F32), lw=dma((4,)),
         nb=V((L, D), BF), q=V((G, L, GW), BF), k=V((G, L, GW), BF), v=V((G, L, GW), BF),
-        probs=V((heads, L, L), BF), mo=V((L, HW), BF), mr=V((T, R, HW), BF),
-        rm=dma((T, R // piece, G)), sm=dma((L // piece, G)),
+        probs=V((heads, L, L), BF), mo=V((L, HW), BF), mr=V((S_, R, HW), BF),
         second=V((R, D), BF), act=V((T, R, FFh), BF), gpre=V((T, R, FFh), BF),
         mlow=V((R, D), BF), gmid=V((R, D), F32), gst=V((T, R, HW), BF), gx=V((L, HW), BF),
-        sg=dma((T, R // RC)), rg=dma((T, R // RC)),
-        ob=V((R, D), BF), so=dma((FO,)), ro=dma((N, 2)), fo=dma((T, N, 2)),
-        igb=V((R, D), BF), si=dma((FO,)), ri=dma((N, 2)), fi=dma((T, N, 2)),
-        mlp_sum=V((RC, D), F32), sec_sum=V((RC, D), F32),
+        ob=V((R, D), BF), so=dma((FO,)), ro=dma((N, 2)),
+        igb=V((R, D), BF), si=dma((FO,)), ri=dma((N, 2)),
         sv=V((n_all + 1, SR, W), F32), rsv=V((n_all, SR, W), F32),
         sv_ss=dma((n_all,)), sv_rs=dma((n_all,)),
         dk=V((L, GW), F32), dv=V((L, GW), F32), gpb=V((L, 3 * HW), BF),
-        gns=V((max(T - 1, 1), R, D), BF), gnr=V((max(T - 1, 1), R, D), BF),
-        sn=dma((T,)), rn=dma((T,)),
     )
+    if by_chip:
+        scratch.update(
+            sx=dma((N // 2, 2)), fx=dma((N // 2, 2)), sc=dma((N // 2, 2)),
+            wq=V((3 * HW, D), BF), rq=dma((3,)), bq=dma((3 * heads,)), sq=dma((2,)),
+            rw=dma((4, 4)), sw=dma((4, 4)), rm=dma((R // 256, G)), sm=dma((L // 256, G)),
+            mid=V((R, D), F32), bsum=V((T, 8, FFh), F32),
+            mlp_sum=V((R, D), F32), sec_sum=V((R, D), F32),
+            sg=dma((R // RC,)), rg=dma((R // RC,)),
+            fo=dma((N // 2, 2)), fi=dma((N // 2, 2)),
+            gns=V((R, D), BF), gnr=V((R, D), BF), sn=dma((1,)), rn=dma((1,)),
+        )
+    else:
+        scratch.update(
+            sx=dma((N, 2)), fx=dma((T, FO)), sc=dma((N, 2)), rw=dma((4, 4, T)), sw=dma((4, 4, T)),
+            rm=dma((T, R // piece, G)), sm=dma((L // piece, G)),
+            sg=dma((T, R // RC)), rg=dma((T, R // RC)), fo=dma((T, N, 2)), fi=dma((T, N, 2)),
+            mlp_sum=V((RC, D), F32), sec_sum=V((RC, D), F32),
+            gns=V((max(T - 1, 1), R, D), BF), gnr=V((max(T - 1, 1), R, D), BF),
+            sn=dma((T,)), rn=dma((T,)),
+        )
     for name, levels in plans.items():
         scratch[name + "_acc"] = V(leads[name] + (widths[name],), BF)
         scratch[name + "_ss"] = dma((2 * len(levels),))
         scratch[name + "_rs"] = dma((2 * len(levels),))
-        for n, (_, _, _, lead, rows) in enumerate(levels):
-            scratch[f"{name}_buf{n}"] = V((lead, rows, widths[name]), BF)
-    names = [n for n, *_ in ins] + [n for n, _ in outs] + list(scratch)
+        for n, (_, _, kind, lead, rows) in enumerate(levels):
+            if kind == "p":
+                continue
+            scratch[name + "_buf" + str(n)] = V((lead, rows, widths[name]), BF)
+    names = list(ins) + list(outs) + list(scratch)
     results = pl.pallas_call(
-        functools.partial(kernel, cfg, names),
-        out_shape=[s for _, s in outs],
-        in_specs=[s for _, _, s in ins],
+        functools.partial(chip_kernel if by_chip else spread_kernel, cfg, names),
+        out_shape=list(outs.values()),
+        in_specs=[s for _, s in ins.values()],
         out_specs=[vm] * len(outs),
         scratch_shapes=list(scratch.values()),
         compiler_params=pltpu.CompilerParams(
             collective_id=0, has_side_effects=True, vmem_limit_bytes=60 * 2**20
         ),
-    )(*[a for _, a, _ in ins])
-    got = dict(zip([n for n, _ in outs], results))
-    grad_qkv = (
-        got["qkv_fin"]
-        .reshape(D, 3, heads, head_dim)
-        .transpose(0, 2, 1, 3)
-        .reshape(w_qkv.shape)
-        .astype(F32)
-    )
-    gains = got["gains"]
+    )(*[a for a, _ in ins.values()])
+    got = SimpleNamespace(**dict(zip(outs, results)))
+    if by_chip:
+        return finish(got, inputs.shape, w_qkv.shape, (D, HW, FFh, GW, G, head_dim), T)
+    grad_qkv = got.qkv_fin.reshape(D, 3, heads, head_dim).transpose(0, 2, 1, 3)
     return (
-        got["out"].reshape(inputs.shape),
-        got["ig"].reshape(inputs.shape),
-        gains[0],
-        gains[1],
-        grad_qkv,
-        got["out_fin"].astype(F32),
-        gains[2],
-        gains[3],
-        got["up_fin"].astype(F32),
-        got["bias_out"][0],
-        got["down_fin"].astype(F32),
+        got.out.reshape(inputs.shape),
+        got.ig.reshape(inputs.shape),
+        got.grad_ga[0],
+        got.grad_sa[0],
+        grad_qkv.reshape(w_qkv.shape).astype(F32),
+        got.out_fin.astype(F32),
+        got.grad_gm[0],
+        got.grad_sm[0],
+        got.up_fin.astype(F32),
+        got.bias_out[0],
+        got.down_fin.astype(F32),
     )
 
 

time: 201 us -> 121 us (0.60)
  Pallas kernels: 184 us -> 120 us
  local copies, waits for them, and re-layouts: 10.4 us -> 0 us
  other arithmetic: 4.03 us -> 0 us
    pallas_call x1 -> x2, Pallas kernels: 184 us -> 120 us  [the longest x1 114 us: body(): pl.pallas_call(functools.partial(chip_kernel if by_chip else spread_kerne...]
    convert_element_type x3 -> x0, other arithmetic: 4.03 us -> none  [the longest x1 1.61 us: body(): got['down_fin'].astype(F32)]
    convert_element_type x2 -> x0, local copies, waits for them, and re-layouts: 2.77 us -> none  [body(): grad_qkv = got['qkv_fin'].reshape(D, 3, heads, head_dim).transpose(0, 2,...]
    unnamed x25 -> x0, local copies, waits for them, and re-layouts: 2.62 us -> none
where the time goes in v2:
time: 121 us
  Pallas kernels  120 us (99%)
    pallas_call x1, Pallas kernels, body(): pl.pallas_call(functools.partial(chip_kernel if by_chip else spread_kerne...  114 us
    pallas_call x1, Pallas kernels, finish(): pl.pallas_call(functools.partial(finish_kernel, sizes), out_shape=[S(got....  6.52 us

profile of v2, /device:TPU:0, one launch (start us, length us, event | category | flops | bytes accessed | tf_op | source)
XLA Modules:
  0.0 120.9 jit_solution(2779665091810473788)
XLA Ops:
  0.6 113.5 %shard_map.203 = (bf16[8,2,64,512]{3,2,1,0:T(8,128)(2,1)}, bf16[8,2,64,512]{3,2,1,0:T(8,128)(2,1)}, bf16[1024,512]{1,0:T(8,128)(2,1)}, bf16[512,1024]{1,0:T(8,12...) custom-call(bf16[8,2,64,512]{3,2,1,0:T(8,128)(2,1)} %bitcast.20, ...), custom_call_target="tpu_custom_call" | custom-call | tf_op jit(solution)/shard_map/pallas_call | solution.py:1535
  114.2 6.5 %shard_map.204 = (bf16[8,2,64,512]{3,2,1,0:T(8,128)(2,1)}, bf16[8,2,64,512]{3,2,1,0:T(8,128)(2,1)}, f32[1,256]{1,0:T(1,128)}, f32[1,256]{1,0:T(1,128)}, f32[4,19...) custom-call(bf16[8,2,64,512]{3,2,1,0:T(8,128)(2,1)} %get-tuple-eleme, ...), custom_call_target="tpu_custom_call" | custom-call | tf_op jit(solution)/shard_map/pallas_call | solution.py:1360

commit v3 on v2

--- a/solution.py
+++ b/solution.py
@@ -92,21 +92,21 @@
 
 
 ORDERS = {
-    "down0": "yxzZ",
-    "down1": "xzyZ",
-    "up0": "zyxZ",
-    "up1": "yxzZ",
-    "out": "xyzR",
+    "down0": "zxyZ",
+    "down1": "yxzZ",
+    "up0": "yzxZ",
+    "up1": "xyzZ",
+    "out": "yxzZ",
     "qkv0": "yxzZ",
-    "qkv1": "xyzZ",
+    "qkv1": "yxzZ",
 }
 CHUNKS = tuple(ORDERS)
 VECTORS, OUTPUT, INPUT_GRAD, MARK = range(7, 11)
-ORDER = tuple(CHUNKS[n] for n in (2, 3, 0, 1))
+ORDER = tuple(CHUNKS[n] for n in (0, 2, 1, 3))
 SCRIPT = (
-    10, 3, 2, 0, 1, 4, 10, 10, 10, 8, 10, 8, 5, 10, 10, 8, 10, 3, 10, 8, 1, 6, 10, 4, 2, 7, 0,
-    3, 1, 6, 9, 0, 9, 5, 7, 9, 3, 9, 0, 5, 7, 4, 3, 5, 7, 2, 4, 0, 1, 3, 6, 5, 2, 4, 0, 6, 1, 3,
-    5, 3, 2, 0, 4, 1, 0, 5, 6, 4, 5, 2, 7, 6, 1, 1, 4, 4, 2, 2, 6, 6,
+    10, 0, 10, 2, 3, 1, 10, 10, 10, 10, 10, 10, 10, 10, 10, 2, 5, 6, 10, 1, 3, 5, 4, 1, 2, 9, 6,
+    5, 2, 0, 9, 3, 5, 7, 1, 4, 6, 3, 0, 4, 5, 0, 9, 9, 2, 1, 4, 6, 8, 5, 3, 8, 1, 7, 0, 4, 2, 8,
+    5, 3, 6, 4, 1, 8, 7, 0, 6, 7, 5, 2, 4, 1, 3, 0, 6, 4, 3, 2, 0, 7, 6,
 )
 
 
@@ -117,7 +117,7 @@
         self.lead, self.rows = acc.shape[0], acc.shape[1]
         self.toff, self.roff = 0, 0
         self.marks = []
-        self.copy = None
+        self.copy = self.result = None
         self.steps = []
         count = len(levels)
         for n in range(count):
@@ -211,6 +211,8 @@
 
     def close(self):
         self.copy.wait()
+        if self.result is not None:
+            self.result.start()
 
     def tick(self):
         if self.steps:
@@ -831,9 +833,10 @@
     pl.semaphore_wait(bar, len(peers))
 
     frames = (i, 2 * N - 1 - i)
+    hops = [0, Z // 2] + [p for p in range(1, Z) if p != Z // 2]
 
     def deal(src_ref, dst_ref, spot, ss, rs):
-        for p in range(Z):
+        for p in hops:
             zz = lax.rem(z + p, Z)
             for h in (0, 1):
                 src = src_ref.at[2 * zz + t, h]
@@ -903,8 +906,9 @@
         arrived(weight_part(name, 1 - t, other_core), rw.at[n, 2])
         arrived(weight_part(name, 1 - t, other_both), rw.at[n, 3])
 
-    RB = min(256, R)
-    nb, qb_, kb_, vb_ = ref.nb, ref.q, ref.k, ref.v
+    RB = 2 * tok
+    nb, qa, ka, va = ref.nb, ref.q, ref.k, ref.v
+    live = ref.live[clip]
     vec = (ref.gain_attn, ref.shift_attn, ref.gain_mlp, ref.shift_mlp)
 
     def project(start):
@@ -913,11 +917,20 @@
         normed = (xhat * vec[0][...] + vec[1][...]).astype(BF)
         nb[rows, :] = normed
         packed = dot(normed, wqkv[...], NT)
-        for g in range(G):
+        side = lax.broadcasted_iota(jnp.int32, (RB, GW), 1)
+        frame = (start + lax.broadcasted_iota(jnp.int32, (RB, GW), 0)) // PATCH
+        for n in range(G * HG):
+            g, h = n // HG, n % HG
+            mine = side // head_dim == h
+            other = side - (1 - h) * head_dim
             lo = g * GW
-            qb_[g, rows, :] = (packed[:, lo : lo + GW].astype(BF).astype(F32) * scale).astype(BF)
-            kb_[g, rows, :] = packed[:, HW + lo : HW + lo + GW].astype(BF)
-            vb_[g, rows, :] = packed[:, 2 * HW + lo : 2 * HW + lo + GW].astype(BF)
+            query = packed[:, lo : lo + GW].astype(BF).astype(F32) * scale
+            key = packed[:, HW + lo : HW + lo + GW]
+            value = packed[:, 2 * HW + lo : 2 * HW + lo + GW]
+            hidden = (other < L // PATCH) & ((frame > other) | (frame >= live))
+            qa[n, rows, :] = jnp.where(mine, query, jnp.where(frame == other, 1.0, 0.0)).astype(BF)
+            ka[n, rows, :] = jnp.where(mine, key, jnp.where(hidden, -1e30, 0.0)).astype(BF)
+            va[n, rows, :] = jnp.where(mine, value, 1.0).astype(BF)
 
     @pl.when(kap != t)
     def _():
@@ -927,42 +940,39 @@
         kap != t, wqkv.at[first_half], wqkv.at[first_half], ref.sq.at[1], rq.at[2], beside
     )
     weights_second("w_out")
-    for p in range(Z):
-        for core in (0, 1):
-            j = 2 * lax.rem(z + p, Z) + core
-            f = j * (1 - kap) + (2 * N - 1 - j) * kap
-            part = xb.at[row_ds(f * tok, tok)]
-            arrived(part, rx.at[f])
-            go(part, part, ref.fx.at[p, core], rx.at[f], mate)
-
-    @pl.when(kap != t)
-    def _():
-        arrived(wqkv.at[other_half], rq.at[2])
-
-    for k in range(R // RB):
-        project(kap * R + k * RB)
-    for k in range(FO):
-        f = (1 - kap) * FO + k
-        arrived(xb.at[row_ds(f * tok, tok)], rx.at[f])
-    for k in range(R // RB):
-        project((1 - kap) * R + k * RB)
-
-    live = ref.live[clip]
+    def first_row(p, core):
+        far = 2 * lax.rem(z + Z - p, Z)
+        return (far * (1 - core) + (2 * N - 2 - far) * core) * tok
+
+    for p in hops:
+        for n in range(2):
+            row = first_row(p, kap) + n * tok
+            part = xb.at[row_ds(row, tok)]
+            arrived(part, rx.at[row // tok])
+            go(part, part, ref.fx.at[p, n], rx.at[row // tok], mate)
+        if p == 0:
+
+            @pl.when(kap != t)
+            def _():
+                arrived(wqkv.at[other_half], rq.at[2])
+
+        if p != hops[-1]:
+            project(first_row(p, kap))
+    for p in hops:
+        if p == hops[-1]:
+            project(first_row(p, kap))
+        for n in range(2):
+            row = first_row(p, 1 - kap) + n * tok
+            arrived(xb.at[row_ds(row, tok)], rx.at[row // tok])
+        project(first_row(p, 1 - kap))
+
     probs, mo, mr = ref.probs, ref.mo, ref.mr
     rm, sm = ref.rm, ref.sm
     NQ = L // QB
-    lane = lax.broadcasted_iota(jnp.int32, (QB, GW), 1) // head_dim
-
-    def pick(parts):
-        out = parts[0]
-        for a in range(1, HG):
-            out = jnp.where(lane == a, parts[a], out)
-        return out
-
-    def only(values, a):
-        if HG == 1:
-            return values
-        return jnp.where(lane == a, values, jnp.zeros_like(values))
+    lane = lax.broadcasted_iota(jnp.int32, (QB, GW), 1)
+
+    def pick(first, second):
+        return jnp.where(lane < head_dim, first, second)
 
     def hand_over(qb, g):
         row = qb * QB
@@ -978,39 +988,31 @@
 
         go_if(kap != s, src, dst, sm.at[qb, g], rm.at[off // QB, g], mate)
 
-    def mask_shift(qb):
+    def attend_block(qb, g):
         K = (qb + 1) * QB
-        row_frame = (qb * QB + lax.broadcasted_iota(jnp.int32, (QB, K), 0)) // PATCH
-        col_frame = lax.broadcasted_iota(jnp.int32, (QB, K), 1) // PATCH
-        allowed = (col_frame <= row_frame) & (col_frame < live)
-        return jnp.where(allowed, 0.0, -1e30)
-
-    def attend_block(qb, g, shift):
-        K = (qb + 1) * QB
-        rows = pl.ds(qb * QB, QB)
-        qv = qb_[g, rows, :]
-        kv = kb_[g, pl.ds(0, K), :]
-        vv = vb_[g, pl.ds(0, K), :]
-        outs = []
-        for a in range(HG):
-            scores = dot(only(qv, a), kv, NT) + shift
+        rows, keys = pl.ds(qb * QB, QB), pl.ds(0, K)
+        outs, sums = [], []
+        for n in range(g * HG, (g + 1) * HG):
+            scores = dot(qa[n, rows, :], ka[n, keys, :], NT)
             top = jnp.max(scores, axis=-1, keepdims=True)
-            weights = jnp.exp(scores - top)
-            total = jnp.sum(weights, axis=-1, keepdims=True)
-            prob = (weights * (1.0 / total)).astype(BF)
-            probs[g * HG + a, rows, pl.ds(0, K)] = prob
-            outs.append(dot(prob, vv))
-        mo[rows, pl.ds(g * GW, GW)] = pick(outs).astype(BF)
+            weights = jnp.exp(scores - top).astype(BF)
+            probs[n, rows, keys] = weights
+            both = dot(weights, va[n, keys, :])
+            outs.append(both)
+            sums.append(pltpu.roll(both, head_dim, 1))
+        inverse = 1.0 / pick(*sums)
+        lanes = pl.ds(g * GW, GW)
+        ref.inv[rows, lanes] = inverse
+        mo[rows, lanes] = (pick(*outs) * inverse).astype(BF)
 
     pumps = {
         (0, 0): functools.partial(weights_second, "w_up"),
-        (1, 1): functools.partial(weights_second, "w_down"),
-        (2, 0): functools.partial(weights_third, "w_out"),
+        (2, 0): functools.partial(weights_second, "w_down"),
+        (2, 1): functools.partial(weights_third, "w_out"),
     }
     for qb in range(NQ):
-        shift = mask_shift(qb)
         for g in range(G):
-            attend_block(qb, g, shift)
+            attend_block(qb, g)
             hand_over(qb, g)
             if (qb, g) in pumps:
                 pumps[qb, g]()
@@ -1022,7 +1024,7 @@
     mid, bsum, sv = ref.mid, ref.bsum, ref.sv
     mlp_sum, sec_sum = ref.mlp_sum, ref.sec_sum
     RC = min(256, R)
-    FT = min(512, FFh)
+    FT = 2 * FFh // len(cfg.order)
     c0 = 0.7978845608028654
 
     def middle_rows(c):
@@ -1035,11 +1037,11 @@
         xhat, _ = norm_parts(middle)
         second[rows, :] = (xhat * vec[2][...] + vec[3][...]).astype(BF)
 
-    def feed_forward(s, c, first):
+    def feed_forward(s, c, tiles, first):
         rows = pl.ds(c * RC, RC)
         sec = second[rows, :]
         cot = cb[rows, :]
-        for j in range(FFh // FT):
+        for j in tiles:
             cols = pl.ds(j * FT, FT)
             pre = dot(sec, wuf[s, :, cols]) + bf_[s, 0:1, cols]
             gact = dot(cot, wdf[s, cols, :], NT)
@@ -1083,9 +1085,9 @@
             gst[s, rows, :] = dot(low, wof[s], NT).astype(BF)
 
     def give_back(buf, dst_ref, ss, rs, k):
-        f = kap * FO + k
-        j = f * (1 - kap) + (2 * N - 1 - f) * kap
-        src = buf.at[pl.ds(k * tok, tok)]
+        j = 2 * lax.rem(z + hops[k // 2], Z) + k % 2
+        f = j * (1 - kap) + (2 * N - 1 - j) * kap
+        src = buf.at[row_ds((f - kap * FO) * tok, tok)]
         dst, sem = dst_ref.at[clip, kap], rs.at[clip, kap]
 
         @pl.when(j == i)
@@ -1096,7 +1098,7 @@
 
     def pass_on(dst_ref, fs, rs, p):
         for h in (0, 1):
-            cc = 2 * lax.rem(z + p, Z) + t
+            cc = 2 * lax.rem(z + Z - hops[p], Z) + t
             part = dst_ref.at[cc, h]
             arrived(part, rs.at[cc, h])
             go(part, part, fs.at[p, h], rs.at[cc, h], mirror)
@@ -1107,32 +1109,22 @@
                 cc = 2 * p + 1 - t
                 arrived(dst_ref.at[cc, h], rs.at[cc, h])
 
-    down_fin, up_fin = ref.down_fin, ref.up_fin
-    fins = {
-        "down0": down_fin.at[pl.ds(0, FFh // 2)],
-        "down1": down_fin.at[pl.ds(FFh // 2, FFh // 2)],
-        "up0": up_fin.at[pl.ds(0, D // 2)],
-        "up1": up_fin.at[pl.ds(D // 2, D // 2)],
-        "out": ref.out_fin,
-        "qkv0": ref.qkv_fin.at[0],
-        "qkv1": ref.qkv_fin.at[1],
-    }
     reduces = {}
     for name, levels in cfg.plans.items():
         bufs = [getattr(ref, name + "_buf" + str(n), None) for n in range(len(levels))]
         reduces[name] = Reduce(
-            levels, getattr(ref, name + "_acc"), fins[name], bufs, getattr(ref, name + "_ss"),
-            getattr(ref, name + "_rs"), place,
+            levels, getattr(ref, name + "_acc"), getattr(ref, name + "_fin"), bufs,
+            getattr(ref, name + "_ss"), getattr(ref, name + "_rs"), place,
         )
+        to, sem = getattr(ref, name + "_sum"), ref.end.at[len(reduces) - 1]
+        reduces[name].result = pltpu.make_async_copy(reduces[name].fin, to, sem)
 
     def grad_wide(name, s):
-        k = int(name[-1])
+        cols = pl.ds(int(name[-1]) * FT, FT)
         if name[0] == "d":
-            cols = pl.ds(k * (FFh // 2), FFh // 2)
             getattr(ref, name + "_acc")[s] = dot(act[s, :, cols], cb[...], TN).astype(BF)
         else:
-            cols = pl.ds(k * (D // 2), D // 2)
-            getattr(ref, name + "_acc")[s] = dot(second[:, cols], gpre[s], TN).astype(BF)
+            getattr(ref, name + "_acc")[s] = dot(second[...], gpre[s, :, cols], TN).astype(BF)
 
     rsv = ref.rsv
     everyone = [("ctx", b) for b in bits_of(N)] + [("dp", b) for b in bits_of(DP)]
@@ -1185,16 +1177,20 @@
             rows, lanes = pl.ds(c * RC, RC), pl.ds(g * GW, GW)
             arrived(mr.at[1 - kap, rows, lanes], rm.at[c, g])
         middle_rows(c)
-        feed_forward(t, c, True)
-        if c == 0:
-            weights_third("w_up")
+        feed_forward(t, c, range(FFh // FT), True)
+        weights_third("w_up" if c == 0 else "w_down")
     for name in cfg.order:
         grad_wide(name, t)
-    weights_third("w_down")
     weights_ready("w_up")
     weights_ready("w_down")
-    for c in range(R // RC):
-        feed_forward(1 - t, c, False)
+    for j in range(FFh // FT):
+        for c in range(R // RC):
+            feed_forward(1 - t, c, (j,), False)
+        run_script()
+        for name in cfg.order:
+            if name[-1] == str(j):
+                grad_wide(name, 1 - t)
+                reduces[name].tick()
     sv[0, 4:5, 0:FFh] = bsum[0, 0:1, :]
     sv[0, 5:6, 0:FFh] = bsum[1, 0:1, :]
     sg, rg = ref.sg, ref.rg
@@ -1207,12 +1203,10 @@
     for k in range(FO):
         give_back(ob, out_ref, ref.so, ref.ro, k)
 
-    for name in cfg.order:
-        grad_wide(name, 1 - t)
-        reduces[name].tick()
     for s in range(T):
         ref.out_acc[s] = dot(mr[s], mlow[...], TN).astype(BF)
     reduces["out"].tick()
+    run_script()
     for c in range(R // RC):
         arrived(gx.at[row_ds((1 - kap) * R + c * RC, RC, 64)], rg.at[c])
 
@@ -1223,39 +1217,40 @@
         rows = pl.ds(qb * QB, QB)
         keys = pl.ds(0, K)
         lanes = pl.ds(g * GW, GW)
-        grad = gx[rows, lanes]
-        prod = grad.astype(F32) * mo[rows, lanes].astype(F32)
-        qv = qb_[g, rows, :]
-        kv = kb_[g, keys, :]
-        vv = vb_[g, keys, :]
+        grad = gx[rows, lanes].astype(F32) * ref.inv[rows, lanes]
+        prod = grad * mo[rows, lanes].astype(F32)
         outs = []
-        dk_sum = dv_sum = None
-        for a in range(HG):
-            delta = jnp.sum(only(prod, a), axis=-1, keepdims=True)
-            goa = only(grad, a)
-            prob = probs[g * HG + a, rows, keys]
-            gprob = dot(goa, vv, NT)
-            gs = (prob.astype(F32) * (gprob - delta)).astype(BF)
-            outs.append(dot(gs, kv))
-            dk_part = dot(gs, only(qv, a), TN)
-            dv_part = dot(prob, goa, TN)
-            dk_sum = dk_part if dk_sum is None else dk_sum + dk_part
-            dv_sum = dv_part if dv_sum is None else dv_sum + dv_part
-        gpb[rows, lanes] = (pick(outs) * scale).astype(BF)
-        if qb == NQ - 1:
-            dk[keys, :] = dk_sum
-            dv[keys, :] = dv_sum
-        else:
-            dk[keys, :] = dk[keys, :] + dk_sum
-            dv[keys, :] = dv[keys, :] + dv_sum
-
-    run_script()
+        for n in range(g * HG, (g + 1) * HG):
+            h = n - g * HG
+            mine = lane // head_dim == h
+            other = lane - (1 - h) * head_dim
+            delta = jnp.sum(jnp.where(mine, prod, 0.0), axis=-1, keepdims=True)
+            high = delta.astype(BF).astype(F32)
+            rest = jnp.where(other == 0, -high, jnp.where(other == 1, high - delta, 0.0))
+            grads = jnp.where(mine, grad, rest).astype(BF)
+            prob = probs[n, rows, keys]
+            gs = (prob.astype(F32) * dot(grads, va[n, keys, :], NT)).astype(BF)
+            outs.append(dot(gs, ka[n, keys, :]))
+            dk_part = dot(gs, qa[n, rows, :], TN)
+            dv_part = dot(prob, grads, TN)
+            if qb == NQ - 1:
+                dk[h, keys, :] = dk_part
+                dv[h, keys, :] = dv_part
+            else:
+                dk[h, keys, :] = dk[h, keys, :] + dk_part
+                dv[h, keys, :] = dv[h, keys, :] + dv_part
+        gpb[rows, lanes] = (pick(*outs) * scale).astype(BF)
+
+    def key_parts(g):
+        first = lax.broadcasted_iota(jnp.int32, (L, GW), 1) < head_dim
+        for b, acc in ((1, dk), (2, dv)):
+            gpb[:, pl.ds(b * HW + g * GW, GW)] = jnp.where(first, acc[0], acc[1]).astype(BF)
+
     for g in range(G):
         for qb in reversed(range(NQ)):
             attend_back_block(g, qb)
             if qb == 0:
-                gpb[:, pl.ds(HW + g * GW, GW)] = dk[...].astype(BF)
-                gpb[:, pl.ds(2 * HW + g * GW, GW)] = dv[...].astype(BF)
+                key_parts(g)
                 for b in range(3):
                     getattr(ref, "qkv" + str(g) + "_acc")[kap, pl.ds(b * GW, GW), :] = dot(
                         gpb[:, pl.ds(b * HW + g * GW, GW)], nb[...], TN
@@ -1292,66 +1287,66 @@
 
     take_rest(out_ref, ref.ro)
     take_rest(ig_ref, ref.ri)
+    for chunk in reduces.values():
+        chunk.result.wait()
     for done in sends:
         done()
 
 
 def finish_kernel(sizes, *refs):
-    D, HW, FFh, GW, G, head_dim = sizes
-    ins, outs, scratch = refs[:11], refs[11:22], refs[22:]
-    out, ig, ga, sa, qkv, wo, gm, sm, up, bias, down = ins
-    b_out, b_ig, b_qkv, b_wo, b_up, b_down, f_qkv, f_wo, f_up, f_down, sem = scratch
+    D, HW, FFh, GW, G, head_dim, tiles = sizes
+    count = 8 + 2 * tiles + G
+    out, ig, ga, sa, gm, sm, bias, wo, *wide = refs[:count]
+    outs = refs[count : count + 11]
+    b_out, b_ig, b_wo, b_down, b_up, b_qkv, f_qkv, f_wo, f_up, f_down, sem = refs[count + 11 :]
+    downs, ups, qkvs = wide[:tiles], wide[tiles : 2 * tiles], wide[2 * tiles :]
     moves = []
 
-    def move(n, src, dst):
-        copy = pltpu.make_async_copy(src, dst, sem.at[n])
+    def move(src, dst):
+        copy = pltpu.make_async_copy(src, dst, sem.at[len(moves)])
         copy.start()
         moves.append(copy)
         return copy
 
-    half = down.shape[0] // 2
-    reads = [
-        move(0, down.at[pl.ds(0, half)], b_down.at[pl.ds(0, half)]),
-        move(1, down.at[pl.ds(half, half)], b_down.at[pl.ds(half, half)]),
-        move(2, up.at[pl.ds(0, D // 2)], b_up.at[pl.ds(0, D // 2)]),
-        move(3, up.at[pl.ds(D // 2, D // 2)], b_up.at[pl.ds(D // 2, D // 2)]),
-        move(4, wo, b_wo),
-        move(5, qkv, b_qkv),
-        move(11, out, b_out),
-        move(12, ig, b_ig),
-    ]
-    parts = (
-        (b_down, f_down, outs[10], 0, half),
-        (b_down, f_down, outs[10], half, half),
-        (b_up, f_up, outs[8], 0, D // 2),
-        (b_up, f_up, outs[8], D // 2, D // 2),
-        (b_wo, f_wo, outs[5], 0, HW),
-    )
-    for n, (src, mid, dst, off, rows) in enumerate(parts):
+    reads = [move(src, b_down.at[n]) for n, src in enumerate(downs)]
+    reads += [move(src, b_up.at[n]) for n, src in enumerate(ups)]
+    reads += [move(wo, b_wo)] + [move(src, b_qkv.at[g]) for g, src in enumerate(qkvs)]
+    reads += [move(out, b_out), move(ig, b_ig)]
+    part = FFh // tiles
+    for n in range(tiles):
         reads[n].wait()
-        at = pl.ds(off, rows)
-        mid[at, :] = src[at, :].astype(F32)
-        move(6 + n, mid.at[at], dst.at[at])
-    for n, (src, dst) in enumerate(((ga, 2), (sa, 3), (gm, 6), (sm, 7), (bias, 9))):
+        at = pl.ds(n * part, part)
+        f_down[at, :] = b_down[n].astype(F32)
+        move(f_down.at[at], outs[10].at[at])
+    for n in range(tiles):
+        reads[tiles + n].wait()
+        at = pl.ds(n * part, part)
+        f_up[:, at] = b_up[n].astype(F32)
+        move(f_up.at[:, at], outs[8].at[:, at])
+    reads[2 * tiles].wait()
+    f_wo[...] = b_wo[...].astype(F32)
+    move(f_wo, outs[5])
+    for n, src, dst in ((-2, b_out, 0), (-1, b_ig, 1)):
+        reads[n].wait()
+        move(src, outs[dst])
+    for src, dst in ((ga, 2), (sa, 3), (gm, 6), (sm, 7), (bias, 9)):
         outs[dst][...] = src[...]
-    reads[6].wait()
-    move(14, b_out, outs[0])
-    reads[7].wait()
-    move(15, b_ig, outs[1])
-    reads[5].wait()
+    pair = GW // head_dim
     for g in range(G):
-        for a in range(GW // head_dim):
+        reads[2 * tiles + 1 + g].wait()
+        for h in range(pair):
             for b in range(3):
-                f_qkv[g * (GW // head_dim) + a, pl.ds(b * head_dim, head_dim), :] = b_qkv[
-                    g, pl.ds(b * GW + a * head_dim, head_dim), :
+                f_qkv[g * pair + h, pl.ds(b * head_dim, head_dim), :] = b_qkv[
+                    g, pl.ds(b * GW + h * head_dim, head_dim), :
                 ].astype(F32)
-    move(13, f_qkv, outs[4])
+        at = pl.ds(g * pair, pair)
+        move(f_qkv.at[at], outs[4].at[at])
     for copy in moves[len(reads) :]:
         copy.wait()
 
 
 def finish(got, layout, qkv_shape, sizes, T):
-    D, HW, FFh, GW, G, head_dim = sizes
+    D, HW, FFh, GW, G, head_dim, tiles = sizes
     vm = pl.BlockSpec(memory_space=pltpu.VMEM)
     hbm = pl.BlockSpec(memory_space=pl.ANY)
     S, V = jax.ShapeDtypeStruct, pltpu.VMEM
@@ -1363,22 +1358,23 @@
             S(got.out.shape, BF), S(got.ig.shape, BF), small, small, S(by_head, F32),
             S((HW, D), F32), small, small, S((D, FFh), F32), S((1, FFh), F32), S((FFh, D), F32),
         ],
-        in_specs=[hbm, hbm, vm, vm, hbm, hbm, vm, vm, hbm, vm, hbm],
+        in_specs=[hbm] * 2 + [vm] * 5 + [hbm] * (1 + 2 * tiles + G),
         out_specs=[hbm, hbm, vm, vm, hbm, hbm, vm, vm, hbm, vm, hbm],
         scratch_shapes=[
-            V(got.out.shape, BF), V(got.ig.shape, BF), V((G, 3 * GW, D), BF), V((HW, D), BF), V((D, FFh), BF), V((FFh, D), BF),
-            V(by_head, F32), V((HW, D), F32), V((D, FFh), F32), V((FFh, D), F32),
-            pltpu.SemaphoreType.DMA((16,)),
+            V(got.out.shape, BF), V(got.ig.shape, BF), V((HW, D), BF),
+            V((tiles, FFh // tiles, D), BF), V((tiles, D, FFh // tiles), BF),
+            V((G, 3 * GW, D), BF), V(by_head, F32), V((HW, D), F32), V((D, FFh), F32),
+            V((FFh, D), F32), pltpu.SemaphoreType.DMA((8 + 4 * tiles + 2 * G,)),
         ],
         compiler_params=pltpu.CompilerParams(vmem_limit_bytes=60 * 2**20),
     )(
-        got.out, got.ig, got.grad_ga, got.grad_sa, got.qkv_fin, got.out_fin, got.grad_gm,
-        got.grad_sm, got.up_fin, got.bias_out, got.down_fin,
+        got.out, got.ig, got.grad_ga, got.grad_sa, got.grad_gm, got.grad_sm, got.bias_out,
+        got.out_sum, *[getattr(got, n + "_sum") for n in CHUNKS if n != "out"],
     )
     out, ig, ga, sa, qkv, wo, gm, sm, up, bias, down = results
     return (
-        out.reshape(layout), ig.reshape(layout), ga[0], sa[0], qkv.transpose(2, 0, 1), wo, gm[0], sm[0], up, bias[0],
-        down,
+        out.reshape(layout), ig.reshape(layout), ga[0], sa[0], qkv.transpose(2, 0, 1), wo, gm[0],
+        sm[0], up, bias[0], down,
     )
 
 
@@ -1404,7 +1400,7 @@
     GW = min(128, HW)
     FFh = w_up.shape[1]
     L = 2 * N * tok
-    by_chip = T == 2 and HW == 256 and N >= 8 and N % 2 == 0 and C == N and DP == 2 and L % 512 == 0
+    by_chip = T == 2 and HW == 256 and head_dim == 64 and N == 8 and tok == PATCH and N % 2 == 0 and C == N and DP == 2 and FFh == 2 * D
     S_ = 2 if by_chip else T
     R = L // S_
     cfg = SimpleNamespace(
@@ -1422,13 +1418,13 @@
         }
         cfg.plans = plans = {}
         cfg.script, cfg.order = SCRIPT, ORDER
-        leads, widths = {}, {}
+        leads, widths, tiles = {}, {}, len(ORDER) // 2
         for name, order in ORDERS.items():
             begin = [("ctx", 1, "p")] if name[0] == "q" else core
             if name[0] == "d":
-                leads[name], widths[name] = (T, FFh // 2), D
+                leads[name], widths[name] = (T, FFh // tiles), D
             elif name[0] == "u":
-                leads[name], widths[name] = (T, D // 2), FFh
+                leads[name], widths[name] = (T, D), FFh // tiles
             elif name[0] == "o":
                 leads[name], widths[name] = (T, HW), D
             else:
@@ -1467,18 +1463,19 @@
         bias=(up_bias.reshape(1, FFh), vm),
     )
     S = jax.ShapeDtypeStruct
-    outs = dict(
-        out=S((C, 2, tok, D), BF),
-        ig=S((C, 2, tok, D), BF),
-        down_fin=S((FFh, D), BF),
-        up_fin=S((D, FFh), BF),
-        out_fin=S((HW, D), BF),
-        qkv_fin=S((G, 3 * GW, D) if by_chip else (D, 3 * HW), BF),
-        grad_ga=S((1, D // T), F32),
-        grad_sa=S((1, D // T), F32),
-        grad_gm=S((1, D // T), F32),
-        grad_sm=S((1, D // T), F32),
-        bias_out=S((1, FFh), F32),
+    outs = dict(out=S((C, 2, tok, D), BF), ig=S((C, 2, tok, D), BF))
+    if by_chip:
+        for name in plans:
+            outs[name + "_sum"] = S((leads[name][1], widths[name]), BF)
+    else:
+        outs.update(
+            down_fin=S((FFh, D), BF), up_fin=S((D, FFh), BF), out_fin=S((HW, D), BF),
+            qkv_fin=S((D, 3 * HW), BF),
+        )
+    large = len(outs)
+    vector = S((1, D // T), F32)
+    outs.update(
+        grad_ga=vector, grad_sa=vector, grad_gm=vector, grad_sm=vector, bias_out=S((1, FFh), F32)
     )
     W = max(D, FFh)
     SR = -(-(4 + T) // 8) * 8
@@ -1493,7 +1490,7 @@
         cb=V((R, D), BF), rc=dma((FO,)),
         w_out_full=V((T, HW, D), BF), w_up_full=V((T, D, FFh), BF),
         w_down_full=V((T, FFh, D), BF), bias_full=V((T, 1, FFh), F32), lw=dma((4,)),
-        nb=V((L, D), BF), q=V((G, L, GW), BF), k=V((G, L, GW), BF), v=V((G, L, GW), BF),
+        nb=V((L, D), BF),
         probs=V((heads, L, L), BF), mo=V((L, HW), BF), mr=V((S_, R, HW), BF),
         second=V((R, D), BF), act=V((T, R, FFh), BF), gpre=V((T, R, FFh), BF),
         mlow=V((R, D), BF), gmid=V((R, D), F32), gst=V((T, R, HW), BF), gx=V((L, HW), BF),
@@ -1501,10 +1498,12 @@
         igb=V((R, D), BF), si=dma((FO,)), ri=dma((N, 2)),
         sv=V((n_all + 1, SR, W), F32), rsv=V((n_all, SR, W), F32),
         sv_ss=dma((n_all,)), sv_rs=dma((n_all,)),
-        dk=V((L, GW), F32), dv=V((L, GW), F32), gpb=V((L, 3 * HW), BF),
+        gpb=V((L, 3 * HW), BF),
     )
     if by_chip:
         scratch.update(
+            q=V((heads, L, GW), BF), k=V((heads, L, GW), BF), v=V((heads, L, GW), BF),
+            inv=V((L, HW), F32), dk=V((2, L, GW), F32), dv=V((2, L, GW), F32),
             sx=dma((N // 2, 2)), fx=dma((N // 2, 2)), sc=dma((N // 2, 2)),
             wq=V((3 * HW, D), BF), rq=dma((3,)), bq=dma((3 * heads,)), sq=dma((2,)),
             rw=dma((4, 4)), sw=dma((4, 4)), rm=dma((R // 256, G)), sm=dma((L // 256, G)),
@@ -1512,10 +1511,12 @@
             mlp_sum=V((R, D), F32), sec_sum=V((R, D), F32),
             sg=dma((R // RC,)), rg=dma((R // RC,)),
             fo=dma((N // 2, 2)), fi=dma((N // 2, 2)),
-            gns=V((R, D), BF), gnr=V((R, D), BF), sn=dma((1,)), rn=dma((1,)),
+            gns=V((R, D), BF), gnr=V((R, D), BF), sn=dma((1,)), rn=dma((1,)), end=dma((len(plans),)),
         )
     else:
         scratch.update(
+            q=V((G, L, GW), BF), k=V((G, L, GW), BF), v=V((G, L, GW), BF),
+            dk=V((L, GW), F32), dv=V((L, GW), F32),
             sx=dma((N, 2)), fx=dma((T, FO)), sc=dma((N, 2)), rw=dma((4, 4, T)), sw=dma((4, 4, T)),
             rm=dma((T, R // piece, G)), sm=dma((L // piece, G)),
             sg=dma((T, R // RC)), rg=dma((T, R // RC)), fo=dma((T, N, 2)), fi=dma((T, N, 2)),
@@ -1525,6 +1526,8 @@
         )
     for name, levels in plans.items():
         scratch[name + "_acc"] = V(leads[name] + (widths[name],), BF)
+        if by_chip:
+            scratch[name + "_fin"] = V((leads[name][1], widths[name]), BF)
         scratch[name + "_ss"] = dma((2 * len(levels),))
         scratch[name + "_rs"] = dma((2 * len(levels),))
         for n, (_, _, kind, lead, rows) in enumerate(levels):
@@ -1536,7 +1539,7 @@
         functools.partial(chip_kernel if by_chip else spread_kernel, cfg, names),
         out_shape=list(outs.values()),
         in_specs=[s for _, s in ins.values()],
-        out_specs=[vm] * len(outs),
+        out_specs=[hbm if by_chip else vm] * large + [vm] * (len(outs) - large),
         scratch_shapes=list(scratch.values()),
         compiler_params=pltpu.CompilerParams(
             collective_id=0, has_side_effects=True, vmem_limit_bytes=60 * 2**20
@@ -1544,7 +1547,7 @@
     )(*[a for a, _ in ins.values()])
     got = SimpleNamespace(**dict(zip(outs, results)))
     if by_chip:
-        return finish(got, inputs.shape, w_qkv.shape, (D, HW, FFh, GW, G, head_dim), T)
+        return finish(got, inputs.shape, w_qkv.shape, (D, HW, FFh, GW, G, head_dim, tiles), T)
     grad_qkv = got.qkv_fin.reshape(D, 3, heads, head_dim).transpose(0, 2, 1, 3)
     return (
         got.out.reshape(inputs.shape),

time: 121 us -> 117 us (0.967)
  Pallas kernels: 120 us -> 116 us
    pallas_call x1, Pallas kernels: 114 us -> 110 us  [body(): pl.pallas_call(functools.partial(chip_kernel if by_chip else spread_kerne...]
where the time goes in v3:
time: 117 us
  Pallas kernels  116 us (99%)
    pallas_call x1, Pallas kernels, body(): pl.pallas_call(functools.partial(chip_kernel if by_chip else spread_kerne...  110 us
    pallas_call x1, Pallas kernels, finish(): pl.pallas_call(functools.partial(finish_kernel, sizes), out_shape=[S(got....  6.53 us

profile of v3, /device:TPU:0, one launch (start us, length us, event | category | flops | bytes accessed | tf_op | source)
XLA Modules:
  0.0 117.0 jit_solution(142590343384894483)
XLA Ops:
  0.6 109.6 %shard_map.203 = (bf16[8,2,64,512]{3,2,1,0:T(8,128)(2,1)}, bf16[8,2,64,512]{3,2,1,0:T(8,128)(2,1)}, bf16[512,512]{1,0:T(8,128)(2,1)}, bf16[512,512]{1,0:T(8,128)...) custom-call(bf16[8,2,64,512]{3,2,1,0:T(8,128)(2,1)} %bitcast.20, ...), custom_call_target="tpu_custom_call" | custom-call | tf_op jit(solution)/shard_map/pallas_call | solution.py:1538
  110.3 6.5 %shard_map.204 = (bf16[8,2,64,512]{3,2,1,0:T(8,128)(2,1)}, bf16[8,2,64,512]{3,2,1,0:T(8,128)(2,1)}, f32[1,256]{1,0:T(1,128)}, f32[1,256]{1,0:T(1,128)}, f32[4,19...) custom-call(bf16[8,2,64,512]{3,2,1,0:T(8,128)(2,1)} %get-tuple-eleme, ...), custom_call_target="tpu_custom_call" | custom-call | tf_op jit(solution)/shard_map/pallas_call | solution.py:1355

commit v4 on v3

--- a/solution.py
+++ b/solution.py
@@ -809,8 +809,14 @@
 
         sends.append(done)
 
+    vec = [ref.vecs.at[n] for n in range(4)]
+    vec_loads = []
+    for n, src in enumerate((ref.gain_attn, ref.shift_attn, ref.gain_mlp, ref.shift_mlp)):
+        vec_loads.append(pltpu.make_async_copy(src, vec[n], ref.vl.at[n]))
+        vec_loads[-1].start()
+
     bar = pltpu.get_barrier_semaphore()
-    peers = [{"ctx": lax.rem(i + p, N)} for p in range(1, N)]
+    peers = [{"ctx": lax.rem(i + p, N)} for p in (4, 3, 5, 2, 6, 1, 7)]
     peers += [mirror] + [{"dp": flip(d, b)} for b in bits_of(DP)]
     for peer in peers:
         pl.semaphore_signal(bar, inc=1, device_id=peer, device_id_type=MESH)
@@ -909,7 +915,8 @@
     RB = 2 * tok
     nb, qa, ka, va = ref.nb, ref.q, ref.k, ref.v
     live = ref.live[clip]
-    vec = (ref.gain_attn, ref.shift_attn, ref.gain_mlp, ref.shift_mlp)
+    for load in vec_loads:
+        load.wait()
 
     def project(start):
         rows = row_ds(start, RB, 64)
@@ -1145,7 +1152,25 @@
             copy.start()
             vec_copy.append(copy)
         else:
-            vec_copy.append(None)
+            small_results()
+
+    vec_out = []
+
+    def small_results():
+        last = sv[len(everyone)]
+        part = D // T
+        gains = last[0:4, 0:part]
+        bias = last[4:5, 0:FFh]
+        for s in range(1, T):
+            gains = jnp.where(t == s, last[0:4, s * part : (s + 1) * part], gains)
+            bias = jnp.where(t == s, last[4 + s : 5 + s, 0:FFh], bias)
+        for n, to in enumerate((ref.grad_ga, ref.grad_sa, ref.grad_gm, ref.grad_sm)):
+            ref.gain_sums[n] = gains[n : n + 1, :]
+            vec_out.append(pltpu.make_async_copy(ref.gain_sums.at[n], to, ref.vo.at[n]))
+        ref.bias_sums[...] = bias
+        vec_out.append(pltpu.make_async_copy(ref.bias_sums, ref.bias_out, ref.vo.at[4]))
+        for copy in vec_out:
+            copy.start()
 
     out_done, ig_done = [], []
     script = list(cfg.script)
@@ -1180,7 +1205,8 @@
         feed_forward(t, c, range(FFh // FT), True)
         weights_third("w_up" if c == 0 else "w_down")
     for name in cfg.order:
-        grad_wide(name, t)
+        if name[-1] == "0":
+            grad_wide(name, t)
     weights_ready("w_up")
     weights_ready("w_down")
     for j in range(FFh // FT):
@@ -1189,6 +1215,8 @@
         run_script()
         for name in cfg.order:
             if name[-1] == str(j):
+                if j > 0:
+                    grad_wide(name, t)
                 grad_wide(name, 1 - t)
                 reduces[name].tick()
     sv[0, 4:5, 0:FFh] = bsum[0, 0:1, :]
@@ -1274,21 +1302,12 @@
         give_back(igb, ig_ref, ref.si, ref.ri, k)
     vec_step()
     run_script()
-    last = sv[len(everyone)]
-    part = D // T
-    gains = last[0:4, 0:part]
-    bias = last[4:5, 0:FFh]
-    for s in range(1, T):
-        gains = jnp.where(t == s, last[0:4, s * part : (s + 1) * part], gains)
-        bias = jnp.where(t == s, last[4 + s : 5 + s, 0:FFh], bias)
-    for n, got in enumerate((ref.grad_ga, ref.grad_sa, ref.grad_gm, ref.grad_sm)):
-        got[...] = gains[n : n + 1, :]
-    ref.bias_out[...] = bias
-
     take_rest(out_ref, ref.ro)
     take_rest(ig_ref, ref.ri)
     for chunk in reduces.values():
         chunk.result.wait()
+    for copy in vec_out:
+        copy.wait()
     for done in sends:
         done()
 
@@ -1298,7 +1317,9 @@
     count = 8 + 2 * tiles + G
     out, ig, ga, sa, gm, sm, bias, wo, *wide = refs[:count]
     outs = refs[count : count + 11]
-    b_out, b_ig, b_wo, b_down, b_up, b_qkv, f_qkv, f_wo, f_up, f_down, sem = refs[count + 11 :]
+    (
+        b_out, b_ig, b_wo, b_down, b_up, b_qkv, f_qkv, f_wo, f_up, f_down, b_vec, b_bias, sem,
+    ) = refs[count + 11 :]
     downs, ups, qkvs = wide[:tiles], wide[tiles : 2 * tiles], wide[2 * tiles :]
     moves = []
 
@@ -1311,6 +1332,10 @@
     reads = [move(src, b_down.at[n]) for n, src in enumerate(downs)]
     reads += [move(src, b_up.at[n]) for n, src in enumerate(ups)]
     reads += [move(wo, b_wo)] + [move(src, b_qkv.at[g]) for g, src in enumerate(qkvs)]
+    vectors = ((ga, b_vec.at[0], 2), (sa, b_vec.at[1], 3), (gm, b_vec.at[2], 6))
+    vectors += ((sm, b_vec.at[3], 7), (bias, b_bias, 9))
+    small = len(reads)
+    reads += [move(src, mid) for src, mid, _ in vectors]
     reads += [move(out, b_out), move(ig, b_ig)]
     part = FFh // tiles
     for n in range(tiles):
@@ -1329,8 +1354,9 @@
     for n, src, dst in ((-2, b_out, 0), (-1, b_ig, 1)):
         reads[n].wait()
         move(src, outs[dst])
-    for src, dst in ((ga, 2), (sa, 3), (gm, 6), (sm, 7), (bias, 9)):
-        outs[dst][...] = src[...]
+    for n, (_, mid, dst) in enumerate(vectors):
+        reads[small + n].wait()
+        move(mid, outs[dst])
     pair = GW // head_dim
     for g in range(G):
         reads[2 * tiles + 1 + g].wait()
@@ -1347,7 +1373,6 @@
 
 def finish(got, layout, qkv_shape, sizes, T):
     D, HW, FFh, GW, G, head_dim, tiles = sizes
-    vm = pl.BlockSpec(memory_space=pltpu.VMEM)
     hbm = pl.BlockSpec(memory_space=pl.ANY)
     S, V = jax.ShapeDtypeStruct, pltpu.VMEM
     small = S((1, D // T), F32)
@@ -1358,13 +1383,14 @@
             S(got.out.shape, BF), S(got.ig.shape, BF), small, small, S(by_head, F32),
             S((HW, D), F32), small, small, S((D, FFh), F32), S((1, FFh), F32), S((FFh, D), F32),
         ],
-        in_specs=[hbm] * 2 + [vm] * 5 + [hbm] * (1 + 2 * tiles + G),
-        out_specs=[hbm, hbm, vm, vm, hbm, hbm, vm, vm, hbm, vm, hbm],
+        in_specs=[hbm] * (8 + 2 * tiles + G),
+        out_specs=[hbm] * 11,
         scratch_shapes=[
             V(got.out.shape, BF), V(got.ig.shape, BF), V((HW, D), BF),
             V((tiles, FFh // tiles, D), BF), V((tiles, D, FFh // tiles), BF),
             V((G, 3 * GW, D), BF), V(by_head, F32), V((HW, D), F32), V((D, FFh), F32),
-            V((FFh, D), F32), pltpu.SemaphoreType.DMA((8 + 4 * tiles + 2 * G,)),
+            V((FFh, D), F32), V((4, 1, D // T), F32), V((1, FFh), F32),
+            pltpu.SemaphoreType.DMA((18 + 4 * tiles + 2 * G,)),
         ],
         compiler_params=pltpu.CompilerParams(vmem_limit_bytes=60 * 2**20),
     )(
@@ -1448,19 +1474,20 @@
 
     vm = pl.BlockSpec(memory_space=pltpu.VMEM)
     hbm = pl.BlockSpec(memory_space=pl.ANY)
+    near = hbm if by_chip else vm
     ins = dict(
         x=(x, hbm),
         cot=(cot, hbm),
         live=(live_frames, pl.BlockSpec(memory_space=pltpu.SMEM)),
-        gain_attn=(gain_attn.reshape(1, D), vm),
-        shift_attn=(shift_attn.reshape(1, D), vm),
-        gain_mlp=(gain_mlp.reshape(1, D), vm),
-        shift_mlp=(shift_mlp.reshape(1, D), vm),
+        gain_attn=(gain_attn.reshape(1, D), near),
+        shift_attn=(shift_attn.reshape(1, D), near),
+        gain_mlp=(gain_mlp.reshape(1, D), near),
+        shift_mlp=(shift_mlp.reshape(1, D), near),
         w_qkv=(wq, hbm if by_chip else vm),
         w_out=(w_out, hbm),
         w_up=(w_up, hbm),
         w_down=(w_down, hbm),
-        bias=(up_bias.reshape(1, FFh), vm),
+        bias=(up_bias.reshape(1, FFh), near),
     )
     S = jax.ShapeDtypeStruct
     outs = dict(out=S((C, 2, tok, D), BF), ig=S((C, 2, tok, D), BF))
@@ -1472,7 +1499,6 @@
             down_fin=S((FFh, D), BF), up_fin=S((D, FFh), BF), out_fin=S((HW, D), BF),
             qkv_fin=S((D, 3 * HW), BF),
         )
-    large = len(outs)
     vector = S((1, D // T), F32)
     outs.update(
         grad_ga=vector, grad_sa=vector, grad_gm=vector, grad_sm=vector, bias_out=S((1, FFh), F32)
@@ -1512,6 +1538,8 @@
             sg=dma((R // RC,)), rg=dma((R // RC,)),
             fo=dma((N // 2, 2)), fi=dma((N // 2, 2)),
             gns=V((R, D), BF), gnr=V((R, D), BF), sn=dma((1,)), rn=dma((1,)), end=dma((len(plans),)),
+            vecs=V((4, 1, D), F32), vl=dma((4,)), gain_sums=V((4, 1, D // T), F32),
+            bias_sums=V((1, FFh), F32), vo=dma((5,)),
         )
     else:
         scratch.update(
@@ -1539,7 +1567,7 @@
         functools.partial(chip_kernel if by_chip else spread_kernel, cfg, names),
         out_shape=list(outs.values()),
         in_specs=[s for _, s in ins.values()],
-        out_specs=[hbm if by_chip else vm] * large + [vm] * (len(outs) - large),
+        out_specs=[hbm if by_chip else vm] * len(outs),
         scratch_shapes=list(scratch.values()),
         compiler_params=pltpu.CompilerParams(
             collective_id=0, has_side_effects=True, vmem_limit_bytes=60 * 2**20

time: 117 us -> 115 us (0.983)
  Pallas kernels: 116 us -> 114 us
where the time goes in v4:
time: 115 us
  Pallas kernels  114 us (99%)
    pallas_call x1, Pallas kernels, body(): pl.pallas_call(functools.partial(chip_kernel if by_chip else spread_kerne...  109 us
    pallas_call x1, Pallas kernels, finish(): pl.pallas_call(functools.partial(finish_kernel, sizes), out_shape=[S(got....  5.45 us

profile of v4, /device:TPU:0, one launch (start us, length us, event | category | flops | bytes accessed | tf_op | source)
XLA Modules:
  0.0 115.1 jit_solution(4492955605964415704)
XLA Ops:
  0.6 108.9 %shard_map.203 = (bf16[8,2,64,512]{3,2,1,0:T(8,128)(2,1)}, bf16[8,2,64,512]{3,2,1,0:T(8,128)(2,1)}, bf16[512,512]{1,0:T(8,128)(2,1)}, bf16[512,512]{1,0:T(8,128)...) custom-call(bf16[8,2,64,512]{3,2,1,0:T(8,128)(2,1)} %bitcast.20, ...), custom_call_target="tpu_custom_call" | custom-call | tf_op jit(solution)/shard_map/pallas_call | solution.py:1566
  109.5 5.5 %shard_map.204 = (bf16[8,2,64,512]{3,2,1,0:T(8,128)(2,1)}, bf16[8,2,64,512]{3,2,1,0:T(8,128)(2,1)}, f32[1,256]{1,0:T(1,128)}, f32[1,256]{1,0:T(1,128)}, f32[4,19...) custom-call(bf16[8,2,64,512]{3,2,1,0:T(8,128)(2,1)} %get-tuple-eleme, ...), custom_call_target="tpu_custom_call" | custom-call | tf_op jit(solution)/shard_map/pallas_call | solution.py:1380

commit v5 on v4

--- a/solution.py
+++ b/solution.py
@@ -971,6 +971,8 @@
         for n in range(2):
             row = first_row(p, 1 - kap) + n * tok
             arrived(xb.at[row_ds(row, tok)], rx.at[row // tok])
+        if p == hops[-1]:
+            weights_second("w_up")
         project(first_row(p, 1 - kap))
 
     probs, mo, mr = ref.probs, ref.mo, ref.mr
@@ -1013,8 +1015,7 @@
         mo[rows, lanes] = (pick(*outs) * inverse).astype(BF)
 
     pumps = {
-        (0, 0): functools.partial(weights_second, "w_up"),
-        (2, 0): functools.partial(weights_second, "w_down"),
+        (1, 1): functools.partial(weights_second, "w_down"),
         (2, 1): functools.partial(weights_third, "w_out"),
     }
     for qb in range(NQ):
@@ -1174,9 +1175,12 @@
 
     out_done, ig_done = [], []
     script = list(cfg.script)
+    old_sends = []
 
     def run_script():
         while script:
+            for _ in range(min(3, len(old_sends))):
+                old_sends.pop(0)()
             item = script.pop(0)
             if item == MARK:
                 return
@@ -1301,6 +1305,8 @@
     for k in range(FO):
         give_back(igb, ig_ref, ref.si, ref.ri, k)
     vec_step()
+    old_sends += sends[: -FO]
+    del sends[: -FO]
     run_script()
     take_rest(out_ref, ref.ro)
     take_rest(ig_ref, ref.ri)
@@ -1308,7 +1314,7 @@
         chunk.result.wait()
     for copy in vec_out:
         copy.wait()
-    for done in sends:
+    for done in old_sends + sends:
         done()
 
 
@@ -1329,6 +1335,7 @@
         moves.append(copy)
         return copy
 
+    ends = [move(out, b_out), move(ig, b_ig)]
     reads = [move(src, b_down.at[n]) for n, src in enumerate(downs)]
     reads += [move(src, b_up.at[n]) for n, src in enumerate(ups)]
     reads += [move(wo, b_wo)] + [move(src, b_qkv.at[g]) for g, src in enumerate(qkvs)]
@@ -1336,7 +1343,9 @@
     vectors += ((sm, b_vec.at[3], 7), (bias, b_bias, 9))
     small = len(reads)
     reads += [move(src, mid) for src, mid, _ in vectors]
-    reads += [move(out, b_out), move(ig, b_ig)]
+    for copy, src, dst in zip(ends, (b_out, b_ig), outs):
+        copy.wait()
+        move(src, dst)
     part = FFh // tiles
     for n in range(tiles):
         reads[n].wait()
@@ -1347,13 +1356,10 @@
         reads[tiles + n].wait()
         at = pl.ds(n * part, part)
         f_up[:, at] = b_up[n].astype(F32)
-        move(f_up.at[:, at], outs[8].at[:, at])
+    move(f_up, outs[8])
     reads[2 * tiles].wait()
     f_wo[...] = b_wo[...].astype(F32)
     move(f_wo, outs[5])
-    for n, src, dst in ((-2, b_out, 0), (-1, b_ig, 1)):
-        reads[n].wait()
-        move(src, outs[dst])
     for n, (_, mid, dst) in enumerate(vectors):
         reads[small + n].wait()
         move(mid, outs[dst])
@@ -1367,7 +1373,7 @@
                 ].astype(F32)
         at = pl.ds(g * pair, pair)
         move(f_qkv.at[at], outs[4].at[at])
-    for copy in moves[len(reads) :]:
+    for copy in moves[len(reads) + 2 :]:
         copy.wait()
 
 

time: 115 us -> 114 us (level)
  no operation moved by 1% of the time
where the time goes in v5:
time: 114 us
  Pallas kernels  113 us (99%)
    pallas_call x1, Pallas kernels, body(): pl.pallas_call(functools.partial(chip_kernel if by_chip else spread_kerne...  108 us
    pallas_call x1, Pallas kernels, finish(): pl.pallas_call(functools.partial(finish_kernel, sizes), out_shape=[S(got....  4.81 us

profile of v5, /device:TPU:0, one launch (start us, length us, event | category | flops | bytes accessed | tf_op | source)
XLA Modules:
  0.0 113.6 jit_solution(5785869599426570011)
XLA Ops:
  0.6 108.0 %shard_map.203 = (bf16[8,2,64,512]{3,2,1,0:T(8,128)(2,1)}, bf16[8,2,64,512]{3,2,1,0:T(8,128)(2,1)}, bf16[512,512]{1,0:T(8,128)(2,1)}, bf16[512,512]{1,0:T(8,128)...) custom-call(bf16[8,2,64,512]{3,2,1,0:T(8,128)(2,1)} %bitcast.20, ...), custom_call_target="tpu_custom_call" | custom-call | tf_op jit(solution)/shard_map/pallas_call | solution.py:1572
  108.6 4.8 %shard_map.204 = (bf16[8,2,64,512]{3,2,1,0:T(8,128)(2,1)}, bf16[8,2,64,512]{3,2,1,0:T(8,128)(2,1)}, f32[1,256]{1,0:T(1,128)}, f32[1,256]{1,0:T(1,128)}, f32[4,19...) custom-call(bf16[8,2,64,512]{3,2,1,0:T(8,128)(2,1)} %get-tuple-eleme, ...), custom_call_target="tpu_custom_call" | custom-call | tf_op jit(solution)/shard_map/pallas_call | solution.py:1386

commit v6 on v5

--- a/solution.py
+++ b/solution.py
@@ -1206,8 +1206,9 @@
             rows, lanes = pl.ds(c * RC, RC), pl.ds(g * GW, GW)
             arrived(mr.at[1 - kap, rows, lanes], rm.at[c, g])
         middle_rows(c)
-        feed_forward(t, c, range(FFh // FT), True)
+        feed_forward(t, c, (0,), True)
         weights_third("w_up" if c == 0 else "w_down")
+        feed_forward(t, c, range(1, FFh // FT), True)
     for name in cfg.order:
         if name[-1] == "0":
             grad_wide(name, t)

time: 114 us -> 114 us (level)
  no operation moved by 1% of the time
where the time goes in v6:
time: 114 us
  Pallas kernels  113 us (99%)
    pallas_call x1, Pallas kernels, body(): pl.pallas_call(functools.partial(chip_kernel if by_chip else spread_kerne...  108 us
    pallas_call x1, Pallas kernels, finish(): pl.pallas_call(functools.partial(finish_kernel, sizes), out_shape=[S(got....  4.81 us

profile of v6, /device:TPU:0, one launch (start us, length us, event | category | flops | bytes accessed | tf_op | source)
XLA Modules:
  0.0 113.7 jit_solution(17316349838419944039)
XLA Ops:
  0.6 108.1 %shard_map.203 = (bf16[8,2,64,512]{3,2,1,0:T(8,128)(2,1)}, bf16[8,2,64,512]{3,2,1,0:T(8,128)(2,1)}, bf16[512,512]{1,0:T(8,128)(2,1)}, bf16[512,512]{1,0:T(8,128)...) custom-call(bf16[8,2,64,512]{3,2,1,0:T(8,128)(2,1)} %bitcast.20, ...), custom_call_target="tpu_custom_call" | custom-call | tf_op jit(solution)/shard_map/pallas_call | solution.py:1573
  108.7 4.8 %shard_map.204 = (bf16[8,2,64,512]{3,2,1,0:T(8,128)(2,1)}, bf16[8,2,64,512]{3,2,1,0:T(8,128)(2,1)}, f32[1,256]{1,0:T(1,128)}, f32[1,256]{1,0:T(1,128)}, f32[4,19...) custom-call(bf16[8,2,64,512]{3,2,1,0:T(8,128)(2,1)} %get-tuple-eleme, ...), custom_call_target="tpu_custom_call" | custom-call | tf_op jit(solution)/shard_map/pallas_call | solution.py:1387
